TPU v7x, 256 devices: a whole 4x4x8 slice. The times are simulated.
256 devices in a mesh: seq: 32 (over y, z_hi, core), lat: 8 (over z_lo, x).
Axes of the slice: x: 4, y: 4, z: 8 (z_hi: 4, z_lo: 2; z = z_hi * 2 + z_lo), core: 2. Of those that a mesh axis runs over, the one named last changes fastest.
Arguments:
- q_raw: bfloat16 [12288, 2048], P('seq', 'lat'), may hold values from -6 to 6
- k_raw: bfloat16 [12288, 2048], P('seq', 'lat'), may hold values from -6 to 6
- v_raw: bfloat16 [12288, 4096], P('seq', 'lat'), may hold values from -6 to 6
- z_gate: bfloat16 [12288, 4096], P('seq', 'lat'), may hold values from -6 to 6
- beta_raw: float32 [32, 12288], P('lat', 'seq'), may hold values from -9 to 4
- decay_log: float32 [32, 12288], P('lat', 'seq'), may hold values from -1.1 to 0
- conv_q: float32 [4, 2048], P(None, 'lat'), may hold values from -3 to 3
- conv_k: float32 [4, 2048], P(None, 'lat'), may hold values from -3 to 3
- conv_v: float32 [4, 4096], P(None, 'lat'), may hold values from -3 to 3
- norm_gain: float32 [128], replicated, may hold values from 0.1 to 1.9
- w_out: bfloat16 [4096, 2048], P('lat'), may hold values from -0.125 to 0.125
- residual: bfloat16 [12288, 2048], P('seq', 'lat'), may hold values from -24 to 24
- post_gain: float32 [2048], replicated, may hold values from 0.1 to 1.9
- w_enc: bfloat16 [2048, 16384], P('seq', 'lat'), may hold values from -0.125 to 0.125
- b_enc: float32 [16384], P('lat'), may hold values from -4 to 4
- w_dec: bfloat16 [2048, 16384], P('seq', 'lat'), may hold values from -0.09375 to 0.09375
- b_dec: float32 [2048], P('lat'), may hold values from -2 to 2
Outputs:
- layer_out: bfloat16 [12288, 2048], P('seq', 'lat')
All inputs are finite; a program needn't handle non-finite values.
Results may differ from a plain program's by a relative error of at most 0.006.
Values may be sent and summed in bfloat16 or wider, within the bound.
A program may use at most 128 MiB of HBM per device.

v0:
```python
import jax
import jax.numpy as jnp
from jax import lax
from jax.sharding import PartitionSpec as P

DK = 128
VALUE_HEAD_WIDTH = 128
CONV = 4
SPAN = 64


TOP_PRECISION = lax.Precision.HIGHEST
EPSILON = 1e-06


def shifted(block, axis, distance):
    devices = range(lax.axis_size(axis))
    route = [(i - distance, i) for i in devices if i - distance in devices]
    return lax.ppermute(block, axis, route)


def entering(shard, axis, combine, identity):
    devices, position = (lax.axis_size(axis), lax.axis_index(axis))
    everything = jax.tree.map(lambda part: lax.all_gather(part, axis), shard)
    start = jax.tree.map(
        lambda part, zero: jnp.broadcast_to(jnp.asarray(zero, part.dtype), part.shape),
        shard,
        identity,
    )

    def turn(k, before):
        reached = k < position
        new = combine(before, jax.tree.map(lambda part: part[k], everything))
        return jax.tree.map(lambda a, b: jnp.where(reached, a, b), new, before)

    return lax.fori_loop(0, devices, turn, start)


def convolve(padded, weights, tok_count):
    summed = weights[0] * padded[0:tok_count].astype(jnp.float32)
    for tap_index in range(1, weights.shape[0]):
        summed = summed + weights[tap_index] * padded[tap_index : tap_index + tok_count].astype(
            jnp.float32
        )
    return jax.nn.silu(summed)


def unit_heads(flat, head_count):
    shaped = flat.reshape(flat.shape[0], head_count, -1)
    return shaped * lax.rsqrt(jnp.sum(shaped * shaped, axis=2, keepdims=True) + EPSILON)


def to_blocks(tensor, length):
    tok_count, head_count, last_width = tensor.shape
    return tensor.reshape(tok_count // length, length, head_count, last_width).transpose(0, 2, 1, 3)


def head_blocks(tensor, length):
    head_count, tok_count = tensor.shape
    return tensor.reshape(head_count, tok_count // length, length).transpose(1, 0, 2)


def span_step(carry_state, inputs):
    queries, keys_in, values, beta_vals, decays = inputs
    length = queries.shape[1]
    cumulative = jnp.cumsum(decays, axis=1)
    spread = cumulative[:, :, None] - cumulative[:, None, :]
    row_ids = lax.broadcasted_iota(jnp.int32, (length, length), 0)
    col_ids = lax.broadcasted_iota(jnp.int32, (length, length), 1)
    within = jnp.where(col_ids <= row_ids, jnp.exp(jnp.minimum(spread, 0.0)), 0.0)
    before = jnp.where(col_ids < row_ids, within, 0.0)
    key_gram = jnp.einsum("hik,hjk->hij", keys_in, keys_in, precision=TOP_PRECISION)
    system = jnp.eye(length, dtype=jnp.float32) + beta_vals[:, :, None] * key_gram * before
    growth = jnp.exp(cumulative)
    targets = jnp.concatenate(
        [beta_vals[:, :, None] * values, (beta_vals * growth)[:, :, None] * keys_in], axis=2
    )
    solved = lax.linalg.triangular_solve(
        system, targets, left_side=True, lower=True, unit_diagonal=True
    )
    val_width = values.shape[2]
    fresh_vals = solved[:, :, :val_width] - jnp.einsum(
        "hik,hkw->hiw", solved[:, :, val_width:], carry_state, precision=TOP_PRECISION
    )
    scores = jnp.einsum("hik,hjk->hij", queries, keys_in, precision=TOP_PRECISION) * within
    output = growth[:, :, None] * jnp.einsum(
        "hik,hkw->hiw", queries, carry_state, precision=TOP_PRECISION
    )
    output = output + jnp.einsum("hij,hjw->hiw", scores, fresh_vals, precision=TOP_PRECISION)
    remain = jnp.exp(cumulative[:, -1:] - cumulative)
    new_state = jnp.exp(cumulative[:, -1])[:, None, None] * carry_state
    new_state = new_state + jnp.einsum(
        "hik,hiw->hkw", keys_in * remain[:, :, None], fresh_vals, precision=TOP_PRECISION
    )
    return (new_state, output)


def compose(earlier, later):
    joined_map = jnp.einsum("hij,hjk->hik", later[0], earlier[0], precision=TOP_PRECISION)
    joined_shift = (
        jnp.einsum("hij,hjk->hik", later[0], earlier[1], precision=TOP_PRECISION) + later[1]
    )
    return (joined_map, joined_shift)


def per_device(
    q_raw,
    k_raw,
    v_raw,
    z_gate,
    beta_raw,
    decay_log,
    conv_q,
    conv_k,
    conv_v,
    norm_gain,
    w_out,
    residual,
    post_gain,
    w_enc,
    b_enc,
    w_dec,
    b_dec,
):
    tok_rows = q_raw.shape[0]
    key_width = q_raw.shape[1]
    heads = v_raw.shape[1] // VALUE_HEAD_WIDTH
    key_heads = key_width // DK
    joined = jnp.concatenate([q_raw, k_raw, v_raw], axis=1)
    earlier_rows = shifted(joined[tok_rows - (CONV - 1) :], "seq", 1)
    weights = jnp.concatenate([conv_q, conv_k, conv_v], axis=1)
    mixed_conv = convolve(jnp.concatenate([earlier_rows, joined], axis=0), weights, tok_rows)
    queries = unit_heads(mixed_conv[:, :key_width], key_heads) * DK ** (-0.5)
    keys_in = unit_heads(mixed_conv[:, key_width : 2 * key_width], key_heads)
    values = mixed_conv[:, 2 * key_width :].reshape(tok_rows, heads, VALUE_HEAD_WIDTH)
    queries = jnp.repeat(queries, heads // key_heads, axis=1)
    keys_in = jnp.repeat(keys_in, heads // key_heads, axis=1)
    extended = jnp.concatenate([values, jnp.zeros((tok_rows, heads, DK), jnp.float32)], axis=2)
    beta_vals = jax.nn.sigmoid(beta_raw)
    blocks = (
        to_blocks(queries, SPAN),
        to_blocks(keys_in, SPAN),
        to_blocks(extended, SPAN),
        head_blocks(beta_vals, SPAN),
        head_blocks(decay_log, SPAN),
    )
    identity_map = jnp.broadcast_to(jnp.eye(DK, dtype=jnp.float32), (heads, DK, DK))
    zero_shift = jnp.zeros((heads, DK, VALUE_HEAD_WIDTH), jnp.float32)
    start_state = jnp.concatenate([zero_shift, identity_map], axis=2)
    final_state, output_list = lax.scan(span_step, start_state, blocks)
    prior = entering(
        (final_state[:, :, VALUE_HEAD_WIDTH:], final_state[:, :, :VALUE_HEAD_WIDTH]),
        "seq",
        compose,
        (identity_map, zero_shift),
    )
    arriving_input = prior[1]
    delta_out = output_list[..., :VALUE_HEAD_WIDTH] + jnp.einsum(
        "fbgr,bry->fbgy",
        output_list[..., VALUE_HEAD_WIDTH:],
        arriving_input,
        precision=TOP_PRECISION,
    )
    delta_out = delta_out.transpose(0, 2, 1, 3).reshape(tok_rows, heads, VALUE_HEAD_WIDTH)
    squares = jnp.mean(delta_out * delta_out, axis=2, keepdims=True)
    gate_vals = jax.nn.silu(z_gate.reshape(tok_rows, heads, VALUE_HEAD_WIDTH).astype(jnp.float32))
    gated = (delta_out * lax.rsqrt(squares + EPSILON) * norm_gain * gate_vals).astype(jnp.bfloat16)
    gated = gated.reshape(tok_rows, heads * VALUE_HEAD_WIDTH)
    attention = jnp.dot(gated, w_out, preferred_element_type=jnp.float32)
    full_attention = lax.psum(attention, "lat")
    full_residual = lax.all_gather(residual, "lat", axis=1, tiled=True)
    stream = (full_residual.astype(jnp.float32) + full_attention).astype(jnp.bfloat16)
    own_width = residual.shape[1]
    own_stream = lax.dynamic_slice_in_dim(stream, lax.axis_index("lat") * own_width, own_width, 1)
    widened = stream.astype(jnp.float32)
    stream_squares = jnp.mean(widened * widened, axis=1, keepdims=True)
    normed = (widened * lax.rsqrt(stream_squares + EPSILON) * post_gain).astype(jnp.bfloat16)
    preact = jnp.dot(
        normed, lax.all_gather(w_enc, "seq", axis=0, tiled=True), preferred_element_type=jnp.float32
    )
    latents = jax.nn.relu(preact + b_enc).astype(jnp.bfloat16)
    decoded = lax.dot_general(
        latents,
        lax.all_gather(w_dec, "seq", axis=0, tiled=True),
        (((1,), (1,)), ((), ())),
        preferred_element_type=jnp.float32,
    )
    summed = lax.psum_scatter(decoded, "lat", scatter_dimension=1, tiled=True)
    return (own_stream.astype(jnp.float32) + summed + b_dec).astype(jnp.bfloat16)


def solution(mesh):
    return jax.shard_map(
        per_device,
        mesh=mesh,
        in_specs=(
            P("seq", "lat"),
            P("seq", "lat"),
            P("seq", "lat"),
            P("seq", "lat"),
            P("lat", "seq"),
            P("lat", "seq"),
            P(None, "lat"),
            P(None, "lat"),
            P(None, "lat"),
            P(),
            P("lat", None),
            P("seq", "lat"),
            P(),
            P("seq", "lat"),
            P("lat"),
            P("seq", "lat"),
            P("lat"),
        ),
        out_specs=P("seq", "lat"),
        check_vma=False,
    )
```

profile of v0, /device:TPU:4, one launch (start us, length us, event | category | flops | bytes accessed | tf_op | source)
XLA Modules:
  0.0 766.2 jit_solution(17708684172527278)
XLA Ops:
  11.1 2.4 collective-permute-start
  16.6 2.5 divide_multiply_fusion
  21.2 2.0 copy.69
  23.2 1.9 copy.67
  26.3 2.5 concatenate.22.clone
  30.0 189.2 %while.26 = (s32[]{:T(128)}, f32[4,128,256]{2,1,0:T(8,128)S(1)}, f32[6,4,64,256]{3,2,0,1:T(8,128)}, f32[6,4,64]{2,0,1:T(8,128)}, f32[6,4,64,128]{3,2,0,1:T(8,128...) while((s32[]{:T(128)}, f32[4,128,256]{2,1,0:T(8,128)S(1)}, ...), condition=%wide.region_4.5_spmd, body=%wide.region_2.4_spmd.sunk | while | flops 479097152 | bytes 6732193 | solution.py:150
  33.1 21.0 %custom-call.8 = f32[4,1,64,64]{2,3,1,0:T(8,128)} custom-call(f32[4,1,64,64]{3,2,1,0:T(8,128)} %fusion.109), custom_call_target="InvertDiagBlocksLowerTriangular" | custom-call | tf_op jit(solution)/shard_map/while/body/eval_jaxpr/triangular_solve | solution.py:78
  64.6 21.0 %custom-call.8 = f32[4,1,64,64]{2,3,1,0:T(8,128)} custom-call(f32[4,1,64,64]{3,2,1,0:T(8,128)} %fusion.109), custom_call_target="InvertDiagBlocksLowerTriangular" | custom-call | tf_op jit(solution)/shard_map/while/body/eval_jaxpr/triangular_solve | solution.py:78
  96.2 21.0 %custom-call.8 = f32[4,1,64,64]{2,3,1,0:T(8,128)} custom-call(f32[4,1,64,64]{3,2,1,0:T(8,128)} %fusion.109), custom_call_target="InvertDiagBlocksLowerTriangular" | custom-call | tf_op jit(solution)/shard_map/while/body/eval_jaxpr/triangular_solve | solution.py:78
  127.7 21.0 %custom-call.8 = f32[4,1,64,64]{2,3,1,0:T(8,128)} custom-call(f32[4,1,64,64]{3,2,1,0:T(8,128)} %fusion.109), custom_call_target="InvertDiagBlocksLowerTriangular" | custom-call | tf_op jit(solution)/shard_map/while/body/eval_jaxpr/triangular_solve | solution.py:78
  159.3 21.0 %custom-call.8 = f32[4,1,64,64]{2,3,1,0:T(8,128)} custom-call(f32[4,1,64,64]{3,2,1,0:T(8,128)} %fusion.109), custom_call_target="InvertDiagBlocksLowerTriangular" | custom-call | tf_op jit(solution)/shard_map/while/body/eval_jaxpr/triangular_solve | solution.py:78
  190.8 21.0 %custom-call.8 = f32[4,1,64,64]{2,3,1,0:T(8,128)} custom-call(f32[4,1,64,64]{3,2,1,0:T(8,128)} %fusion.109), custom_call_target="InvertDiagBlocksLowerTriangular" | custom-call | tf_op jit(solution)/shard_map/while/body/eval_jaxpr/triangular_solve | solution.py:78
  221.7 88.3 %all-gather.14.cloned.1.call-done = f32[128,128,128]{2,1,0:T(8,128)} async-done(((f32[4,128,128]{2,1,0:T(8,128)}), f32[128,128,128]{2,1,0:T(8,128)}) %all-gather.14.cloned.1.call-update) | async-done | bytes 8388624 | tf_op jit(solution)/shard_map/all_gather | solution.py:24
  310.0 79.6 %all-gather.16.cloned.1.call-done = f32[128,128,128]{2,1,0:T(8,128)} async-done(((f32[4,128,128]{2,1,0:T(8,128)}), f32[128,128,128]{2,1,0:T(8,128)}) %all-gather.16.cloned.1.call-update) | async-done | bytes 8388624 | tf_op jit(solution)/shard_map/all_gather | solution.py:24
  389.6 47.5 %while.27 = (s32[]{:T(128)}, f32[4,128,128]{2,1,0:T(8,128)S(1)}, s32[]{:T(128)}, f32[32,4,128,128]{3,2,1,0:T(8,128)}, f32[32,4,128,128]{3,2,1,0:T(8,128)}, /*index=5*/s32[]{:T(128)}, s32[]{:T(128)}) while((s32[]{:T(128)}, f32[4,128,128]{2,1,0:T(8,128)S(1)}, s32[]{:T(128)}, f32[32,4,128,128]{3,2,1,0:T(8,128)}, ...), condition=%wide.region_6.7_spmd.clone, body=%wide.region_5.6_spmd.clone.sunk | while | flops 100925440 | bytes 1837663 | solution.py:36
  437.1 2.3 multiply_reduce_fusion
  440.6 2.8 fusion.56
  444.9 91.8 %all-reduce.4.cloned.1.call-done = f32[384,2048]{1,0:T(8,128)} async-done(((f32[384,2048]{1,0:T(8,128)}), f32[384,2048]{1,0:T(8,128)}) %all-reduce.4.cloned.1.call-update) | async-done | bytes 3145744 | tf_op jit(solution)/shard_map/psum | solution.py:170
  536.6 2.9 fusion.38
  539.5 79.0 %all-gather.10.cloned.1.call-done = bf16[2048,2048]{1,0:T(8,128)(2,1)} async-done(((bf16[64,2048]{1,0:T(8,128)(2,1)}), bf16[2048,2048]{1,0:T(8,128)(2,1)}) %all-gather.10.cloned.1.call-update) | async-done | bytes 8388624 | tf_op jit(solution)/shard_map/all_gather | solution.py:179
  618.5 79.5 %all-gather.12.cloned.1.call-done = bf16[2048,2048]{1,0:T(8,128)(2,1)} async-done(((bf16[64,2048]{1,0:T(8,128)(2,1)}), bf16[2048,2048]{1,0:T(8,128)(2,1)}) %all-gather.12.cloned.1.call-update) | async-done | bytes 8388624 | tf_op jit(solution)/shard_map/all_gather | solution.py:184
  698.0 14.1 %fusion.54 = f32[384,2048]{1,0:T(8,128)} fusion(bf16[2048,2048]{1,0:T(8,128)(2,1)} %all-gather.12.cloned.1.call-done, bf16[2048,2048]{1,0:T(8,128)(2,1)} %all-gather.10.cloned.1.call-done, bf16[384,2048]{1,0:T(8,128)(2,1)S(1)} %get-tuple-element.224, f32[2048]{0:T(1024)S(1)} %copy-done.17, f32[2048]{0:T(1024)S(1)} %copy-done.18, f32[384]{0:T(512)S(1)} %add_rsqrt_fusion.3), kind=kOutput, calls=%fused_computation.86 | convolution fusion | flops 6447955968 | bytes 21513728 | tf_op jit(solution)/shard_map/dot_general | solution.py:182
  712.2 45.4 %reduce-scatter.2.cloned.1.call-done = f32[384,256]{1,0:T(8,128)} async-done(((f32[384,2048]{1,0:T(8,128)}), f32[384,256]{1,0:T(8,128)}) %reduce-scatter.2.cloned.1.call-update) | async-done | bytes 393232 | tf_op jit(solution)/shard_map/reduce_scatter | solution.py:188
  757.6 1.8 add_convert_fusion.1
  (291 shorter events, 125.7 us)
Async XLA Ops:
  6.5 434.1 %copy-start = (bf16[512,2048]{1,0:T(8,128)(2,1)S(1)}, bf16[512,2048]{1,0:T(8,128)(2,1)}, u32[]{:S(2)}) copy-start(bf16[512,2048]{1,0:T(8,128)(2,1)} %param.31) | copy-start | bytes 6291460
  6.5 303.5 %all-gather.14.cloned.1.call-start = ((), (), s32[]{:S(2)}) async-start(), calls=%async_computation.6 | async-start | bytes 8650752 | tf_op jit(solution)/shard_map/all_gather | solution.py:24
  7.9 5.7 copy-start.12
  7.9 5.6 copy-start.13
  7.9 5.6 copy-start.9
  7.9 5.7 copy-start.10
  7.9 6.4 copy-start.11
  11.1 4.0 collective-permute-start
  88.2 4.2 copy-start.8
  88.2 4.1 copy-start.6
  119.7 4.1 copy-start.8
  119.7 4.1 copy-start.6
  214.3 4.1 copy-start.8
  220.1 169.5 %all-gather.16.cloned.1.call-start = ((), (), s32[]{:S(2)}) async-start(), calls=%async_computation.7 | async-start | bytes 8650752 | tf_op jit(solution)/shard_map/all_gather | solution.py:24
  220.9 224.0 %all-gather.8.cloned.1.call-start = ((), (), s32[]{:S(2)}) async-start(), calls=%async_computation.1 | async-start | bytes 1769472 | tf_op jit(solution)/shard_map/all_gather | solution.py:171
  221.6 315.0 %all-reduce.4.cloned.1.call-start = ((), (), s32[]{:S(2)}) async-start(), calls=%async_computation.2 | async-start | bytes 6291456 | tf_op jit(solution)/shard_map/psum | solution.py:170
  443.4 175.1 %all-gather.10.cloned.1.call-start = ((), (), s32[]{:S(2)}) async-start(), calls=%async_computation.3 | async-start | bytes 8650752 | tf_op jit(solution)/shard_map/all_gather | solution.py:179
  444.0 254.0 %all-gather.12.cloned.1.call-start = ((), (), s32[]{:S(2)}) async-start(), calls=%async_computation.4 | async-start | bytes 8650752 | tf_op jit(solution)/shard_map/all_gather | solution.py:184
  444.6 253.4 %copy-start.17 = (f32[2048]{0:T(1024)S(1)}, f32[2048]{0:T(1024)}, u32[]{:S(2)}) copy-start(f32[2048]{0:T(1024)} %param.35) | copy-start | bytes 24580
  444.6 253.4 %copy-start.18 = (f32[2048]{0:T(1024)S(1)}, f32[2048]{0:T(1024)}, u32[]{:S(2)}) copy-start(f32[2048]{0:T(1024)} %param.33) | copy-start | bytes 24580
  444.6 313.0 %reduce-scatter.2.cloned.1.call-start = ((), (), s32[]{:S(2)}) async-start(), calls=%async_computation.5 | async-start | bytes 3538944 | tf_op jit(solution)/shard_map/reduce_scatter | solution.py:188
  539.5 172.6 %copy-start.3 = (bf16[384,2048]{1,0:T(8,128)(2,1)}, bf16[384,2048]{1,0:T(8,128)(2,1)S(1)}, u32[]{:S(2)}) copy-start(bf16[384,2048]{1,0:T(8,128)(2,1)S(1)} %get-tuple-element.224) | copy-start | bytes 4718596
  712.1 47.2 %copy-start.1 = (bf16[512,2048]{1,0:T(8,128)(2,1)S(1)}, bf16[512,2048]{1,0:T(8,128)(2,1)}, u32[]{:S(2)}) copy-start(bf16[512,2048]{1,0:T(8,128)(2,1)} %param.31) | copy-start | bytes 6291460
  712.1 45.5 %copy-start.14 = (f32[256]{0:T(256)S(1)}, f32[256]{0:T(256)}, u32[]{:S(2)}) copy-start(f32[256]{0:T(256)} %param.37) | copy-start | bytes 3076
  (19 other events, 46.9 us)
Sparse Core Ops, SparseCore 0:
  220.2 89.7 all-gather.13
  312.6 77.0 all-gather.15
  391.4 43.0 all-gather.7
  443.6 93.0 all-reduce.3
  539.0 79.4 all-gather.9
  620.9 77.0 all-gather.11
  712.3 45.2 reduce-scatter.1
where the time goes:
time: 771 us; the launch traced here: 766 us
  waiting for transfers between devices  466 us (60%)
  other arithmetic  149 us (19%)
  matrix products  109 us (14%)
  local copies, waits for them, and re-layouts  24 us (3%)
  between operations  13.8 us (2%)
    all_gather x2, waiting for transfers between devices, entering(): everything = jax.tree.map(lambda part: lax.all_gather(part, axis), shard)  168 us
    another operation x24, other arithmetic, span_step(): lax.linalg.triangular_solve(system, targets, left_side=True, lower=True,...  127 us
    psum x1, waiting for transfers between devices, per_device(): full_attention = lax.psum(attention, 'lat')  91.8 us
    all_gather x1, waiting for transfers between devices, per_device(): lax.all_gather(w_dec, 'seq', axis=0, tiled=True)  79.5 us
    all_gather x1, waiting for transfers between devices, per_device(): lax.all_gather(w_enc, 'seq', axis=0, tiled=True)  79 us
    dot_general x32, matrix products, compose(): jnp.einsum('hij,hjk->hik', later[0], earlier[1], precision=TOP_PRECISION)  45.7 us
    reduce_scatter x1, waiting for transfers between devices, per_device(): summed = lax.psum_scatter(decoded, 'lat', scatter_dimension=1, tiled=True)  45.4 us
  transfers between devices with their start and end apart: 8, of which 6 were waited for; matrix products, arithmetic and copies ran while one was open for 7% of the time, Pallas kernels for 0%

commit v1 on v0

v1 whole, which is shorter than its diff:
```python
import functools

import jax
import jax.numpy as jnp
from jax import lax
from jax.experimental import pallas as pl
from jax.experimental.pallas import tpu as pltpu
from jax.sharding import PartitionSpec as P

F32 = jnp.float32
BF16 = jnp.bfloat16
EPSILON = 1e-06
T = 384
C = 128
H = 4
W = 128
ROW = 8
ROWS = 4
LAT = 8
TOP = lax.Precision.HIGHEST
MESH = pl.DeviceIdType.MESH
VMEM_LIMIT = 56 << 20


def mm(a, b, dims=((1,), (0,))):
    return lax.dot_general(
        a.astype(BF16), b.astype(BF16), (dims, ((), ())), preferred_element_type=F32
    )


def halves(a):
    high = a.astype(BF16)
    return high, (a - high.astype(F32)).astype(BF16)


def mm3(a, b, dims=((1,), (0,))):
    ah, al = a
    bh, bl = b
    dot = lambda x, y: lax.dot_general(x, y, (dims, ((), ())), preferred_element_type=F32)
    return dot(ah, bh) + (dot(ah, bl) + dot(al, bh))


def mm6(a, b, dims=((1,), (0,))):
    return lax.dot_general(a, b, (dims, ((), ())), precision=TOP, preferred_element_type=F32)


def silu(v):
    return v / (1.0 + jnp.exp(-v))


def triangular_inverses(systems, row, col):
    first = ((row & 1) == 1) & (col == row - 1)
    eye = (row == col).astype(F32)
    solved = [eye - jnp.where(first, a, 0.0) for a in systems]
    for level in range(1, 7):
        block_row, block_col = row >> level, col >> level
        mask = ((block_row & 1) == 1) & (block_col == block_row - 1)
        parts = [halves(x) for x in solved]
        below = [mm3(halves(jnp.where(mask, a, 0.0)), x) for a, x in zip(systems, parts)]
        solved = [x - mm3(p, halves(b)) for x, p, b in zip(solved, parts, below)]
    return solved


def remote(src, dst, send, recv, **where):
    return pltpu.make_async_remote_copy(
        src_ref=src,
        dst_ref=dst,
        send_sem=send,
        recv_sem=recv,
        device_id=where,
        device_id_type=MESH,
    )


def mixing_kernel(
    q_ref, k_ref, v_ref, z_ref, bd_ref, wc_ref, gain_ref, wout_ref,
    part_ref,
    halo, pad, qs, ks, vs, ql, ol, comp, acur, msg, slots, prefix, aprefix, tot, tslots, sout, sin,
    hs, hr, ms, mr, ts, tr, ss, sr,
):
    seq = lax.axis_index("seq")
    n_seq = ROW * ROWS
    right, left = lax.rem(seq + 1, n_seq), lax.rem(seq + n_seq - 1, n_seq)
    y, j = seq // ROW, lax.rem(seq, ROW)
    zh, core = j // 2, lax.rem(j, 2)
    base = y * ROW

    barrier = pltpu.get_barrier_semaphore()
    pl.semaphore_signal(barrier, inc=1, device_id={"seq": right}, device_id_type=MESH)
    pl.semaphore_signal(barrier, inc=1, device_id={"seq": left}, device_id_type=MESH)
    for d in range(1, ROW):
        peer = base + lax.rem(j + d, ROW)
        pl.semaphore_signal(barrier, inc=1, device_id={"seq": peer}, device_id_type=MESH)
    for d in range(1, ROWS):
        peer = lax.rem(y + d, ROWS) * ROW + j
        pl.semaphore_signal(barrier, inc=1, device_id={"seq": peer}, device_id_type=MESH)
    pl.semaphore_wait(barrier, 2 + ROW - 1 + ROWS - 1)

    halos = []
    for i, (ref, lo, width) in enumerate(((q_ref, 0, 256), (k_ref, 256, 256), (v_ref, 512, 512))):
        halos.append(
            remote(
                ref.at[pl.ds(T - 16, 16), :],
                halo.at[:, pl.ds(lo, width)],
                hs.at[i], hr.at[i], seq=right,
            )
        )
        halos[-1].start()
        pad[pl.ds(16, T), lo : lo + width] = ref[...].astype(F32)
    for copy in halos:
        copy.wait()
    pad[pl.ds(0, 16), :] = jnp.where(seq == 0, 0.0, halo[...].astype(F32))

    for g in range(8):
        cols = slice(g * W, (g + 1) * W)
        total = wc_ref[0:1, cols] * pad[13 : 13 + T, cols]
        for tap in range(1, 4):
            total = total + wc_ref[tap : tap + 1, cols] * pad[13 + tap : 13 + tap + T, cols]
        total = silu(total)
        if g < 4:
            total = total * lax.rsqrt(jnp.sum(total * total, axis=1, keepdims=True) + EPSILON)
        if g < 2:
            qs[:, cols] = total * (W**-0.5)
        elif g < 4:
            ks[:, (g - 2) * W : (g - 1) * W] = total
        else:
            vs[:, (g - 4) * W : (g - 3) * W] = total

    row = lax.broadcasted_iota(jnp.int32, (C, C), 0)
    col = lax.broadcasted_iota(jnp.int32, (C, C), 1)
    lower = (col <= row).astype(F32)
    upper = (row <= col).astype(F32)
    eye = (row == col).astype(F32)
    ones = jnp.ones((C, C), F32)
    comp[...] = jnp.zeros_like(comp)
    acur[...] = jnp.ones_like(acur)

    def block(c, _):
        rows = pl.ds(pl.multiple_of(c * C, C), C)
        bd = bd_ref[c]
        beta_col = mm6(eye, 1.0 / (1.0 + jnp.exp(-bd)), ((1,), (1,)))
        cum_col = mm6(lower, bd, ((1,), (1,)))
        cum_row = mm6(bd, upper)
        tot_row = mm6(bd, ones)
        systems, scores, keys, queries = [], [], [], []
        for kh in range(2):
            k = ks[rows, kh * W : (kh + 1) * W]
            q = qs[rows, kh * W : (kh + 1) * W]
            kp, qp = halves(k), halves(q)
            gram = mm3(kp, kp, ((1,), (1,)))
            score = mm3(qp, kp, ((1,), (1,)))
            keys.append(k)
            queries.append(q)
            for h in (2 * kh, 2 * kh + 1):
                spread = cum_col[:, 4 + h : 5 + h] - cum_row[4 + h : 5 + h, :]
                within = jnp.where(col <= row, jnp.exp(jnp.minimum(spread, 0.0)), 0.0)
                systems.append(
                    jnp.where(col < row, beta_col[:, h : h + 1] * gram * within, 0.0)
                )
                scores.append(score * within)
        solved = triangular_inverses(systems, row, col)
        key_t = [k.T for k in keys]
        for h in range(H):
            kh = h // 2
            beta = beta_col[:, h : h + 1]
            growth = jnp.exp(cum_col[:, 4 + h : 5 + h])
            v = vs[rows, h * W : (h + 1) * W]
            targets = jnp.concatenate([beta * v, (beta * growth) * keys[kh]], axis=1)
            fresh = mm(solved[h], targets).astype(BF16)
            out = mm(scores[h], fresh)
            q_map = growth * queries[kh] - out[:, W:]
            total = tot_row[4 + h : 5 + h, :]
            decay = jnp.exp(total)
            remain = jnp.exp(total - cum_row[4 + h : 5 + h, :])
            new = mm(key_t[kh] * remain, fresh)
            so_far = comp[h]
            a = acur[h, 0:1, :]
            read = mm(q_map, so_far)
            ql[h, rows, :] = (a * q_map - read[:, W:]).astype(BF16)
            ol[h, rows, :] = out[:, :W] + read[:, :W]
            turned = mm(new[:, W:], so_far)
            decay2 = jnp.concatenate([decay, decay], axis=1)
            comp[h] = (
                decay2 * so_far - turned + jnp.concatenate([new[:, :W], a * new[:, W:]], axis=1)
            )
            acur[h] = jnp.broadcast_to(a * decay, (8, W))
        return 0

    lax.fori_loop(0, T // C, block, 0)

    def split_row(a):
        high = a.astype(BF16).astype(F32)
        mid = (a - high).astype(BF16).astype(F32)
        low = a - high - mid
        r = lax.broadcasted_iota(jnp.int32, (16, W), 0)
        block = jnp.where(r == 0, high, jnp.where(r == 1, mid, jnp.where(r == 2, low, 0.0)))
        return jnp.concatenate([block, block], axis=1).astype(BF16)

    def joined_row(ref):
        return jnp.sum(ref[C : C + 16, :W].astype(F32), axis=0, keepdims=True)

    for h in range(H):
        msg[h, :C, :] = comp[h].astype(BF16)
        msg[h, C:, :] = split_row(acur[h, 0:1, :])

    def to_handler(h):
        return remote(msg.at[h], slots.at[j], ms.at[h], mr.at[j], seq=base + 2 * h)

    for h in range(H):

        @pl.when(j != 2 * h)
        def _():
            to_handler(h).start()

        @pl.when(j == 2 * h)
        def _():
            slots[j] = msg[h]

    def total_to(d):
        peer = lax.rem(y + d, ROWS)
        return remote(tot, tslots.at[y], ts.at[d - 1], tr.at[y], seq=peer * ROW + j)

    def state_to(i):
        return remote(sout.at[i], sin.at[zh], ss.at[i], sr.at[zh], seq=base + i)

    @pl.when(core == 0)
    def _():
        for i in range(ROW):

            @pl.when(i != j)
            def _():
                remote(msg.at[0], slots.at[i], ms.at[0], mr.at[i], seq=base + i).wait_recv()

            maps = slots[i, :C, :]
            a_new = joined_row(slots.at[i])
            if i == 0:
                now, a_now = maps.astype(F32), a_new
            else:
                a_old, old = aprefix[i - 1, 0:1, :], prefix[i - 1]
                turned = mm(maps[:, W:], old)
                new = maps.astype(F32)
                a2 = jnp.concatenate([a_new, a_new], axis=1)
                now = (
                    a2 * old - turned + jnp.concatenate([new[:, :W], a_old * new[:, W:]], axis=1)
                )
                a_now = a_old * a_new
            prefix[i] = now
            aprefix[i] = jnp.broadcast_to(a_now, (8, W))
        tot[:C, :] = prefix[ROW - 1].astype(BF16)
        tot[C:, :] = split_row(aprefix[ROW - 1, 0:1, :])
        for d in range(1, ROWS):
            total_to(d).start()
        tslots[y] = tot[...]
        state = jnp.zeros((C, W), F32)
        for i in range(ROWS):

            @pl.when(i != y)
            def _():
                remote(tot, tslots.at[i], ts.at[0], tr.at[i], seq=i * ROW + j).wait_recv()

            maps = tslots[i]
            later = (
                joined_row(tslots.at[i]) * state
                - mm(maps[:C, W:], state)
                + maps[:C, :W].astype(F32)
            )
            state = jnp.where(i < y, later, state)
        for i in range(ROW):
            if i == 0:
                mine = state
            else:
                mine = (
                    aprefix[i - 1, 0:1, :] * state
                    - mm(prefix[i - 1, :, W:], state)
                    + prefix[i - 1, :, :W]
                )
            sout[i] = mine.astype(BF16)

            @pl.when(i != j)
            def _():
                state_to(i).start()

            @pl.when(i == j)
            def _():
                sin[zh] = sout[i]

    gated = []
    for h in range(H):

        @pl.when(j != 2 * h)
        def _():
            remote(sout.at[0], sin.at[h], ss.at[0], sr.at[h], seq=base + 2 * h).wait_recv()

        delta = ol[h] + mm(ql[h], sin[h])
        squares = jnp.mean(delta * delta, axis=1, keepdims=True)
        gate = silu(z_ref[:, h * W : (h + 1) * W].astype(F32))
        gated.append((delta * lax.rsqrt(squares + EPSILON) * gain_ref[...] * gate).astype(BF16))
    gated = jnp.concatenate(gated, axis=1)
    for lane in range(LAT):
        part_ref[lane] = mm(gated, wout_ref[:, lane * 256 : (lane + 1) * 256]).astype(BF16)

    for h in range(H):

        @pl.when(j != 2 * h)
        def _():
            to_handler(h).wait_send()

    @pl.when(core == 0)
    def _():
        for d in range(1, ROWS):
            total_to(d).wait_send()
        for i in range(ROW):

            @pl.when(i != j)
            def _():
                state_to(i).wait_send()


def mixing(q, k, v, z, bd, wc, gain, wout):
    return pl.pallas_call(
        mixing_kernel,
        out_shape=jax.ShapeDtypeStruct((LAT, T, 256), BF16),
        in_specs=[pl.BlockSpec(memory_space=pltpu.VMEM)] * 8,
        out_specs=pl.BlockSpec(memory_space=pltpu.VMEM),
        scratch_shapes=[
            pltpu.VMEM((16, 1024), BF16),
            pltpu.VMEM((T + 16, 1024), F32),
            pltpu.VMEM((T, 256), F32),
            pltpu.VMEM((T, 256), F32),
            pltpu.VMEM((T, 512), F32),
            pltpu.VMEM((H, T, W), BF16),
            pltpu.VMEM((H, T, W), F32),
            pltpu.VMEM((H, C, 2 * W), F32),
            pltpu.VMEM((H, 8, W), F32),
            pltpu.VMEM((H, C + 16, 2 * W), BF16),
            pltpu.VMEM((ROW, C + 16, 2 * W), BF16),
            pltpu.VMEM((ROW, C, 2 * W), F32),
            pltpu.VMEM((ROW, 8, W), F32),
            pltpu.VMEM((C + 16, 2 * W), BF16),
            pltpu.VMEM((ROWS, C + 16, 2 * W), BF16),
            pltpu.VMEM((ROW, C, W), BF16),
            pltpu.VMEM((H, C, W), BF16),
            pltpu.SemaphoreType.DMA((3,)),
            pltpu.SemaphoreType.DMA((3,)),
            pltpu.SemaphoreType.DMA((H,)),
            pltpu.SemaphoreType.DMA((ROW,)),
            pltpu.SemaphoreType.DMA((ROWS - 1,)),
            pltpu.SemaphoreType.DMA((ROWS,)),
            pltpu.SemaphoreType.DMA((ROW,)),
            pltpu.SemaphoreType.DMA((H,)),
        ],
        compiler_params=pltpu.CompilerParams(
            collective_id=0, has_side_effects=True, vmem_limit_bytes=VMEM_LIMIT
        ),
        cost_estimate=pl.CostEstimate(
            flops=100_000_000_000, bytes_accessed=8_000_000, transcendentals=0
        ),
        name="mixing",
    )(q, k, v, z, bd, wc, gain, wout)


def transcoder_kernel(
    part_ref, res_ref, gain_ref, benc_ref, bdec_ref, wenc_hbm, wdec_hbm,
    out_ref,
    wenc, wdec, arrived, streams, normed, latents, decoded, returned,
    wsem, s1, r1, s2, r2, s3, r3,
):
    me = lax.axis_index("lat")
    load_enc = pltpu.make_async_copy(wenc_hbm, wenc, wsem.at[0])
    load_dec = pltpu.make_async_copy(wdec_hbm, wdec, wsem.at[1])
    load_enc.start()
    load_dec.start()

    barrier = pltpu.get_barrier_semaphore()
    for d in range(1, LAT):
        peer = lax.rem(me + d, LAT)
        pl.semaphore_signal(barrier, inc=1, device_id={"lat": peer}, device_id_type=MESH)
    pl.semaphore_wait(barrier, LAT - 1)

    def peer_at(d):
        return lax.rem(me + d, LAT)

    def scatter(d):
        return remote(part_ref.at[peer_at(d)], arrived.at[me], s1.at[d - 1], r1.at[me], lat=peer_at(d))

    def gather(d):
        return remote(streams.at[me], streams.at[me], s2.at[d - 1], r2.at[me], lat=peer_at(d))

    def scatter_back(d):
        return remote(decoded.at[peer_at(d)], returned.at[me], s3.at[d - 1], r3.at[me], lat=peer_at(d))

    for d in range(1, LAT):
        scatter(d).start()
    attention = part_ref[me].astype(F32)
    for d in range(1, LAT):
        p = peer_at(d)
        remote(part_ref.at[p], arrived.at[p], s1.at[0], r1.at[p], lat=p).wait_recv()
        attention = attention + arrived[p].astype(F32)
    streams[me] = (res_ref[...].astype(F32) + attention).astype(BF16)
    for d in range(1, LAT):
        gather(d).start()
    own = streams[me].astype(F32)
    squares = jnp.sum(own * own, axis=1, keepdims=True)
    for d in range(1, LAT):
        p = peer_at(d)
        remote(streams.at[p], streams.at[p], s2.at[0], r2.at[p], lat=p).wait_recv()
        wide = streams[p].astype(F32)
        squares = squares + jnp.sum(wide * wide, axis=1, keepdims=True)
    scale = lax.rsqrt(squares * (1.0 / 2048.0) + EPSILON)
    for l in range(LAT):
        cols = slice(l * 256, (l + 1) * 256)
        normed[:, cols] = (streams[l].astype(F32) * scale * gain_ref[:, cols]).astype(BF16)
    load_enc.wait()

    def encode(i, _):
        cols = pl.ds(pl.multiple_of(i * 256, 256), 256)
        pre = jnp.dot(normed[...], wenc[:, cols], preferred_element_type=F32) + benc_ref[:, cols]
        latents[:, cols] = jnp.maximum(pre, 0.0).astype(BF16)
        return 0

    lax.fori_loop(0, LAT, encode, 0)
    load_dec.wait()

    def decode(p):
        rows = pl.ds(pl.multiple_of(p * 256, 256), 256)
        return lax.dot_general(
            latents[...], wdec[rows, :], (((1,), (1,)), ((), ())), preferred_element_type=F32
        )

    def decode_step(d, _):
        p = peer_at(d)
        decoded[p] = decode(p).astype(BF16)
        scatter_back(d).start()
        return 0

    lax.fori_loop(1, LAT, decode_step, 0)
    total = decode(me) + streams[me].astype(F32) + bdec_ref[...]
    for d in range(1, LAT):
        p = peer_at(d)
        remote(decoded.at[p], returned.at[p], s3.at[0], r3.at[p], lat=p).wait_recv()
        total = total + returned[p].astype(F32)
    out_ref[...] = total.astype(BF16)
    for d in range(1, LAT):
        scatter(d).wait_send()
        gather(d).wait_send()
        scatter_back(d).wait_send()


def transcoder(part, residual, gain, benc, bdec, wenc, wdec):
    vmem = pl.BlockSpec(memory_space=pltpu.VMEM)
    block = pltpu.VMEM((LAT, T, 256), BF16)
    return pl.pallas_call(
        transcoder_kernel,
        out_shape=jax.ShapeDtypeStruct((T, 256), BF16),
        in_specs=[vmem] * 5 + [pl.BlockSpec(memory_space=pl.ANY)] * 2,
        out_specs=vmem,
        scratch_shapes=[
            pltpu.VMEM((2048, 2048), BF16),
            pltpu.VMEM((2048, 2048), BF16),
            block,
            block,
            pltpu.VMEM((T, 2048), BF16),
            pltpu.VMEM((T, 2048), BF16),
            block,
            block,
            pltpu.SemaphoreType.DMA((2,)),
        ]
        + [pltpu.SemaphoreType.DMA((LAT - 1,)), pltpu.SemaphoreType.DMA((LAT,))] * 3,
        compiler_params=pltpu.CompilerParams(
            collective_id=1, has_side_effects=True, vmem_limit_bytes=VMEM_LIMIT
        ),
        cost_estimate=pl.CostEstimate(
            flops=6_442_450_944, bytes_accessed=20_000_000, transcendentals=0
        ),
        name="transcoder",
    )(part, residual, gain, benc, bdec, wenc, wdec)


def per_device(
    q_raw,
    k_raw,
    v_raw,
    z_gate,
    beta_raw,
    decay_log,
    conv_q,
    conv_k,
    conv_v,
    norm_gain,
    w_out,
    residual,
    post_gain,
    w_enc,
    b_enc,
    w_dec,
    b_dec,
):
    bd = jnp.concatenate([beta_raw, decay_log], axis=0)
    bd = bd.reshape(8, T // C, C).transpose(1, 0, 2)
    wc = jnp.concatenate([conv_q, conv_k, conv_v], axis=1)
    wenc = lax.all_gather(w_enc, "seq", axis=0, tiled=True)
    wdec = lax.all_gather(w_dec, "seq", axis=0, tiled=True)
    part = mixing(q_raw, k_raw, v_raw, z_gate, bd, wc, norm_gain[None, :], w_out)
    return transcoder(
        part, residual, post_gain[None, :], b_enc[None, :], b_dec[None, :], wenc, wdec
    )


def solution(mesh):
    return jax.shard_map(
        per_device,
        mesh=mesh,
        in_specs=(
            P("seq", "lat"),
            P("seq", "lat"),
            P("seq", "lat"),
            P("seq", "lat"),
            P("lat", "seq"),
            P("lat", "seq"),
            P(None, "lat"),
            P(None, "lat"),
            P(None, "lat"),
            P(),
            P("lat", None),
            P("seq", "lat"),
            P(),
            P("seq", "lat"),
            P("lat"),
            P("seq", "lat"),
            P("lat"),
        ),
        out_specs=P("seq", "lat"),
        check_vma=False,
    )
```

time: 771 us -> 264 us (0.34)
  waiting for transfers between devices: 466 us -> 111 us
  other arithmetic: 149 us -> 2.64 us
  Pallas kernels: 0 us -> 135 us
  matrix products: 109 us -> 0 us
  local copies, waits for them, and re-layouts: 24 us -> 1.62 us
    all_gather x5 -> x2, waiting for transfers between devices: 326 us -> 109 us  [the longest x1 81.9 us: per_device(): wdec = lax.all_gather(w_dec, 'seq', axis=0, tiled=True)]
    pallas_call x0 -> x2, Pallas kernels: none -> 135 us  [the longest x1 79.7 us: transcoder(): pl.pallas_call(transcoder_kernel, out_shape=jax.ShapeDtypeStruct((T, 256)...]
    another operation x30 -> x0, other arithmetic: 128 us -> none  [the longest x24 127 us: span_step(): lax.linalg.triangular_solve(system, targets, left_side=True, lower=True,...]
    dot_general x71 -> x0, matrix products: 100 us -> none  [the longest x32 45.7 us: compose(): jnp.einsum('hij,hjk->hik', later[0], earlier[1], precision=TOP_PRECISION)]
    psum x1 -> x0, waiting for transfers between devices: 91.8 us -> none  [per_device(): full_attention = lax.psum(attention, 'lat')]
    reduce_scatter x1 -> x0, waiting for transfers between devices: 45.4 us -> none  [per_device(): summed = lax.psum_scatter(decoded, 'lat', scatter_dimension=1, tiled=True)]
    mul x15 -> x0, other arithmetic: 10.3 us -> none  [the longest x6 6.26 us: span_step(): beta_vals[:, :, None] * values]
    another operation x6 -> x0, matrix products: 8.61 us -> none  [span_step(): lax.linalg.triangular_solve(system, targets, left_side=True, lower=True,...]
  transfers between devices with their start and end apart: 8 -> 2, of which waited for: 6 -> 2; matrix products, arithmetic and copies ran while one was open for 7% -> 1% of each run, Pallas kernels for 0% -> 21%
where the time goes in v1:
time: 264 us
  Pallas kernels  135 us (51%)
  waiting for transfers between devices  111 us (42%)
  between operations  13.4 us (5%)
  other arithmetic  2.64 us (1%)
    all_gather x1, waiting for transfers between devices, per_device(): wdec = lax.all_gather(w_dec, 'seq', axis=0, tiled=True)  81.9 us
    pallas_call x1, Pallas kernels, transcoder(): pl.pallas_call(transcoder_kernel, out_shape=jax.ShapeDtypeStruct((T, 256)...  79.7 us
    pallas_call x1, Pallas kernels, mixing(): pl.pallas_call(mixing_kernel, out_shape=jax.ShapeDtypeStruct((LAT, T, 256...  55.5 us
    all_gather x1, waiting for transfers between devices, per_device(): wenc = lax.all_gather(w_enc, 'seq', axis=0, tiled=True)  27.3 us
  transfers between devices with their start and end apart: 2, of which 2 were waited for; matrix products, arithmetic and copies ran while one was open for 1% of the time, Pallas kernels for 21%

profile of v1, /device:TPU:4, one launch (start us, length us, event | category | flops | bytes accessed | tf_op | source)
XLA Modules:
  0.0 263.5 jit_solution(8255272488512668413)
XLA Ops:
  6.5 0.0 all-gather.3.cloned.1.call-start
  6.5 0.7 all-gather.3.cloned.1.call-update
  7.3 0.0 all-gather.5.cloned.1.call-start
  7.3 0.7 all-gather.5.cloned.1.call-update
  8.0 1.3 maximum_bitcast_fusion.bd_ref
  9.3 1.3 pad_maximum_fusion.wc_ref
  10.7 55.5 %mixing.1.part_ref = bf16[8,384,256]{2,1,0:T(8,128)(2,1)} custom-call(bf16[384,256]{1,0:T(8,128)(2,1)} %q_ref.1, bf16[384,256]{1,0:T(8,128)(2,1)} %k_ref.1, bf16[384,512]{1,0:T(8,128)(2,1)} %v_ref.1, bf16[384,512]{1,0:T(8,128)(2,1)} %z_ref.1, f32[3,8,128]{2,1,0:T(8,128)} %maximum_bitcast_fusion.bd_ref, f32[4,1024]{1,0:T(4,128)} %pad_maximum_fusion.wc_ref, ...), custom_call_target="tpu_custom_call" | custom-call | flops 99999997952 | bytes 8000000 | tf_op jit(solution)/shard_map/mixing/pallas_call | solution.py:320
  66.1 27.3 %all-gather.3.cloned.1.call-done.wenc_hbm = bf16[2048,2048]{1,0:T(8,128)(2,1)} async-done(((bf16[64,2048]{1,0:T(8,128)(2,1)}), bf16[2048,2048]{1,0:T(8,128)(2,1)}) %all-gather.3.cloned.1.call-update) | async-done | bytes 8388624 | tf_op jit(solution)/shard_map/all_gather | solution.py:501
  93.5 81.9 %all-gather.5.cloned.1.call-done.wdec_hbm = bf16[2048,2048]{1,0:T(8,128)(2,1)} async-done(((bf16[64,2048]{1,0:T(8,128)(2,1)}), bf16[2048,2048]{1,0:T(8,128)(2,1)}) %all-gather.5.cloned.1.call-update) | async-done | bytes 8388624 | tf_op jit(solution)/shard_map/all_gather | solution.py:502
  175.3 79.7 %transcoder.1 = bf16[384,256]{1,0:T(8,128)(2,1)} custom-call(bf16[8,384,256]{2,1,0:T(8,128)(2,1)} %mixing.1.part_ref, bf16[384,256]{1,0:T(8,128)(2,1)} %res_ref.1, f32[1,2048]{1,0:T(1,128)} %bitcast.8, f32[1,2048]{1,0:T(1,128)} %bitcast.9, f32[1,256]{1,0:T(1,128)} %bitcast.10, bf16[2048,2048]{1,0:T(8,128)(2,1)} %all-gather.3.cloned.1.call-done.wenc_hbm, ...), custom_call_target="tpu_custom_call" | custom-call | flops 6442450944 | bytes 20000000 | tf_op jit(solution)/shard_map/transcoder/pallas_call | solution.py:452
  255.1 1.6 copy.19
Async XLA Ops:
  6.5 86.9 %all-gather.3.cloned.1.call-start = ((), (), s32[]{:S(2)}) async-start(), calls=%async_computation | async-start | bytes 8650752 | tf_op jit(solution)/shard_map/all_gather | solution.py:501
  7.3 168.1 %all-gather.5.cloned.1.call-start = ((), (), s32[]{:S(2)}) async-start(), calls=%async_computation.1 | async-start | bytes 8650752 | tf_op jit(solution)/shard_map/all_gather | solution.py:502
Sparse Core Ops, SparseCore 0:
  9.9 83.5 all-gather.2
  96.0 79.2 all-gather.4

commit v2 on v1

--- a/solution.py
+++ b/solution.py
@@ -72,13 +72,18 @@
     )
 
 
-def mixing_kernel(
-    q_ref, k_ref, v_ref, z_ref, bd_ref, wc_ref, gain_ref, wout_ref,
-    part_ref,
+def layer_kernel(
+    q_ref, k_ref, v_ref, z_ref, bd_ref, wc_ref, gain_ref,
+    res_ref, pgain_ref, benc_ref, bdec_ref, wout_hbm, wenc_hbm, wdec_hbm,
+    out_ref,
     halo, pad, qs, ks, vs, ql, ol, comp, acur, msg, slots, prefix, aprefix, tot, tslots, sout, sin,
+    wout_ref, wenc, wdec, part_ref, arrived, streams, normed, latents, decoded, returned,
     hs, hr, ms, mr, ts, tr, ss, sr,
+    wsem, s1, r1, s2, r2, s3, r3,
+    gr, cr, cs, z1s, z2s, y1s, y2s,
 ):
     seq = lax.axis_index("seq")
+    me = lax.axis_index("lat")
     n_seq = ROW * ROWS
     right, left = lax.rem(seq + 1, n_seq), lax.rem(seq + n_seq - 1, n_seq)
     y, j = seq // ROW, lax.rem(seq, ROW)
@@ -94,8 +99,80 @@
     for d in range(1, ROWS):
         peer = lax.rem(y + d, ROWS) * ROW + j
         pl.semaphore_signal(barrier, inc=1, device_id={"seq": peer}, device_id_type=MESH)
-    pl.semaphore_wait(barrier, 2 + ROW - 1 + ROWS - 1)
-
+    for d in range(1, LAT):
+        peer = lax.rem(me + d, LAT)
+        pl.semaphore_signal(barrier, inc=1, device_id={"lat": peer}, device_id_type=MESH)
+    pl.semaphore_wait(barrier, 2 + ROW - 1 + ROWS - 1 + LAT - 1)
+
+    full, own_shard = (wenc, wdec), (wenc_hbm, wdec_hbm)
+    sibling = base + 2 * zh + 1 - core
+
+    def shard_id(dy, dz):
+        return lax.rem(y + dy, ROWS) * 4 + lax.rem(zh + dz, 4)
+
+    def shard(a, s, c):
+        return full[a].at[pl.ds(pl.multiple_of((s * 2 + c) * 64, 64), 64), :]
+
+    def seq_at(dy, dz):
+        return shard_id(dy, dz) * 2 + core
+
+    def passed(a, s, sem, to):
+        return remote(shard(a, s, core), shard(a, s, core), sem, gr.at[a, s], seq=to)
+
+    def along_z(a, up):
+        to = seq_at(0, 1 if up else 3)
+        here = shard(a, shard_id(0, 0), core)
+        return remote(own_shard[a], here, z1s.at[a, int(up)], gr.at[a, shard_id(0, 0)], seq=to)
+
+    def along_z_on(a):
+        return passed(a, shard_id(0, 3 if a == 0 else 1), z2s.at[a], seq_at(0, 1 if a == 0 else 3))
+
+    def along_y(a, dz, up):
+        s, to, sem = shard_id(0, dz), seq_at(1 if up else 3, 0), y1s.at[a, dz, int(up)]
+        if dz == 0:
+            return remote(own_shard[a], shard(a, s, core), sem, gr.at[a, s], seq=to)
+        return passed(a, s, sem, to)
+
+    def along_y_on(a, dz):
+        s = shard_id(3 if a == 0 else 1, dz)
+        return passed(a, s, y2s.at[a, dz], seq_at(1 if a == 0 else 3, 0))
+
+    def across(a, dy, dz):
+        s = shard_id(dy, dz)
+        src = own_shard[a] if dy == 0 and dz == 0 else shard(a, s, core)
+        return remote(src, shard(a, s, core), cs.at[a, s], cr.at[a, s], seq=sibling)
+
+    def landed(a, dy, dz):
+        s = shard_id(dy, dz)
+        remote(shard(a, s, core), shard(a, s, core), cs.at[a, s], gr.at[a, s], seq=sibling).wait_recv()
+
+    def landed_across(a, dy, dz):
+        s = shard_id(dy, dz)
+        there = shard(a, s, 1 - core)
+        remote(there, there, cs.at[a, s], cr.at[a, s], seq=sibling).wait_recv()
+
+    def from_z(a, dz):
+        landed(a, 0, dz)
+        along_y(a, dz, True).start()
+        along_y(a, dz, False).start()
+        across(a, 0, dz).start()
+
+    def from_y(a, dz):
+        for dy in (3, 1) if a == 0 else (1, 3):
+            landed(a, dy, dz)
+            if dy == (3 if a == 0 else 1):
+                along_y_on(a, dz).start()
+            across(a, dy, dz).start()
+
+    def from_y_on(a, dz):
+        landed(a, 2, dz)
+        across(a, 2, dz).start()
+
+    loads = [
+        pltpu.make_async_copy(wenc_hbm, shard(0, shard_id(0, 0), core), wsem.at[0]),
+        pltpu.make_async_copy(wdec_hbm, shard(1, shard_id(0, 0), core), wsem.at[1]),
+        pltpu.make_async_copy(wout_hbm, wout_ref, wsem.at[2]),
+    ]
     halos = []
     for i, (ref, lo, width) in enumerate(((q_ref, 0, 256), (k_ref, 256, 256), (v_ref, 512, 512))):
         halos.append(
@@ -107,6 +184,13 @@
         )
         halos[-1].start()
         pad[pl.ds(16, T), lo : lo + width] = ref[...].astype(F32)
+    for a in range(2):
+        for up in (True, False):
+            along_z(a, up).start()
+            along_y(a, 0, up).start()
+        across(a, 0, 0).start()
+    for copy in loads:
+        copy.start()
     for copy in halos:
         copy.wait()
     pad[pl.ds(0, 16), :] = jnp.where(seq == 0, 0.0, halo[...].astype(F32))
@@ -125,6 +209,10 @@
             ks[:, (g - 2) * W : (g - 1) * W] = total
         else:
             vs[:, (g - 4) * W : (g - 3) * W] = total
+
+    from_z(0, 3)
+    along_z_on(0).start()
+    from_z(0, 1)
 
     row = lax.broadcasted_iota(jnp.int32, (C, C), 0)
     col = lax.broadcasted_iota(jnp.int32, (C, C), 1)
@@ -184,6 +272,20 @@
                 decay2 * so_far - turned + jnp.concatenate([new[:, :W], a * new[:, W:]], axis=1)
             )
             acur[h] = jnp.broadcast_to(a * decay, (8, W))
+
+        @pl.when(c == 0)
+        def _():
+            from_z(1, 1)
+            along_z_on(1).start()
+            from_z(1, 3)
+            from_y(0, 0)
+            from_y(1, 0)
+
+        @pl.when(c == 1)
+        def _():
+            from_z(0, 2)
+            from_z(1, 2)
+
         return 0
 
     lax.fori_loop(0, T // C, block, 0)
@@ -215,6 +317,9 @@
         @pl.when(j == 2 * h)
         def _():
             slots[j] = msg[h]
+
+    from_y(0, 1)
+    from_y(0, 3)
 
     def total_to(d):
         peer = lax.rem(y + d, ROWS)
@@ -284,6 +389,9 @@
             def _():
                 sin[zh] = sout[i]
 
+    from_y(1, 1)
+    from_y(1, 3)
+
     gated = []
     for h in range(H):
 
@@ -296,6 +404,8 @@
         gate = silu(z_ref[:, h * W : (h + 1) * W].astype(F32))
         gated.append((delta * lax.rsqrt(squares + EPSILON) * gain_ref[...] * gate).astype(BF16))
     gated = jnp.concatenate(gated, axis=1)
+    for copy in loads:
+        copy.wait()
     for lane in range(LAT):
         part_ref[lane] = mm(gated, wout_ref[:, lane * 256 : (lane + 1) * 256]).astype(BF16)
 
@@ -315,13 +425,103 @@
             def _():
                 state_to(i).wait_send()
 
-
-def mixing(q, k, v, z, bd, wc, gain, wout):
+    def peer_at(d):
+        return lax.rem(me + d, LAT)
+
+    def scatter(d):
+        return remote(part_ref.at[peer_at(d)], arrived.at[me], s1.at[d - 1], r1.at[me], lat=peer_at(d))
+
+    def gather(d):
+        return remote(streams.at[me], streams.at[me], s2.at[d - 1], r2.at[me], lat=peer_at(d))
+
+    def scatter_back(d):
+        return remote(decoded.at[peer_at(d)], returned.at[me], s3.at[d - 1], r3.at[me], lat=peer_at(d))
+
+    for d in range(1, LAT):
+        scatter(d).start()
+    from_y(0, 2)
+    from_y(1, 2)
+    attention = part_ref[me].astype(F32)
+    for d in range(1, LAT):
+        p = peer_at(d)
+        remote(part_ref.at[p], arrived.at[p], s1.at[0], r1.at[p], lat=p).wait_recv()
+        attention = attention + arrived[p].astype(F32)
+    streams[me] = (res_ref[...].astype(F32) + attention).astype(BF16)
+    for d in range(1, LAT):
+        gather(d).start()
+    for dz in range(4):
+        for a in range(2):
+            from_y_on(a, dz)
+    own = streams[me].astype(F32)
+    squares = jnp.sum(own * own, axis=1, keepdims=True)
+    for d in range(1, LAT):
+        p = peer_at(d)
+        remote(streams.at[p], streams.at[p], s2.at[0], r2.at[p], lat=p).wait_recv()
+        wide = streams[p].astype(F32)
+        squares = squares + jnp.sum(wide * wide, axis=1, keepdims=True)
+    scale = lax.rsqrt(squares * (1.0 / 2048.0) + EPSILON)
+    for l in range(LAT):
+        cols = slice(l * 256, (l + 1) * 256)
+        normed[:, cols] = (streams[l].astype(F32) * scale * pgain_ref[:, cols]).astype(BF16)
+    for dy in range(4):
+        for dz in range(4):
+            landed_across(0, dy, dz)
+
+    def encode(i, _):
+        cols = pl.ds(pl.multiple_of(i * 256, 256), 256)
+        pre = jnp.dot(normed[...], wenc[:, cols], preferred_element_type=F32) + benc_ref[:, cols]
+        latents[:, cols] = jnp.maximum(pre, 0.0).astype(BF16)
+        return 0
+
+    lax.fori_loop(0, LAT, encode, 0)
+    for dy in range(4):
+        for dz in range(4):
+            landed_across(1, dy, dz)
+
+    def decode(p):
+        rows = pl.ds(pl.multiple_of(p * 256, 256), 256)
+        return lax.dot_general(
+            latents[...], wdec[rows, :], (((1,), (1,)), ((), ())), preferred_element_type=F32
+        )
+
+    def decode_step(d, _):
+        p = peer_at(d)
+        decoded[p] = decode(p).astype(BF16)
+        scatter_back(d).start()
+        return 0
+
+    lax.fori_loop(1, LAT, decode_step, 0)
+    total = decode(me) + streams[me].astype(F32) + bdec_ref[...]
+    for d in range(1, LAT):
+        p = peer_at(d)
+        remote(decoded.at[p], returned.at[p], s3.at[0], r3.at[p], lat=p).wait_recv()
+        total = total + returned[p].astype(F32)
+    out_ref[...] = total.astype(BF16)
+    for d in range(1, LAT):
+        scatter(d).wait_send()
+        gather(d).wait_send()
+        scatter_back(d).wait_send()
+    for a in range(2):
+        for up in (True, False):
+            along_z(a, up).wait_send()
+        along_z_on(a).wait_send()
+        for dz in range(4):
+            for up in (True, False):
+                along_y(a, dz, up).wait_send()
+            along_y_on(a, dz).wait_send()
+            for dy in range(4):
+                across(a, dy, dz).wait_send()
+
+
+def layer(q, k, v, z, bd, wc, gain, residual, pgain, benc, bdec, wout, wenc, wdec):
+    vmem = pl.BlockSpec(memory_space=pltpu.VMEM)
+    block = pltpu.VMEM((LAT, T, 256), BF16)
+    dma = pltpu.SemaphoreType.DMA
     return pl.pallas_call(
-        mixing_kernel,
-        out_shape=jax.ShapeDtypeStruct((LAT, T, 256), BF16),
-        in_specs=[pl.BlockSpec(memory_space=pltpu.VMEM)] * 8,
-        out_specs=pl.BlockSpec(memory_space=pltpu.VMEM),
+        layer_kernel,
+        out_shape=jax.ShapeDtypeStruct((T, 256), BF16),
+        in_specs=[vmem] * 11 + [pl.BlockSpec(memory_space=pl.ANY)] * 3,
+        out_specs=vmem,
         scratch_shapes=[
             pltpu.VMEM((16, 1024), BF16),
             pltpu.VMEM((T + 16, 1024), F32),
@@ -340,140 +540,34 @@
             pltpu.VMEM((ROWS, C + 16, 2 * W), BF16),
             pltpu.VMEM((ROW, C, W), BF16),
             pltpu.VMEM((H, C, W), BF16),
-            pltpu.SemaphoreType.DMA((3,)),
-            pltpu.SemaphoreType.DMA((3,)),
-            pltpu.SemaphoreType.DMA((H,)),
-            pltpu.SemaphoreType.DMA((ROW,)),
-            pltpu.SemaphoreType.DMA((ROWS - 1,)),
-            pltpu.SemaphoreType.DMA((ROWS,)),
-            pltpu.SemaphoreType.DMA((ROW,)),
-            pltpu.SemaphoreType.DMA((H,)),
-        ],
-        compiler_params=pltpu.CompilerParams(
-            collective_id=0, has_side_effects=True, vmem_limit_bytes=VMEM_LIMIT
-        ),
-        cost_estimate=pl.CostEstimate(
-            flops=100_000_000_000, bytes_accessed=8_000_000, transcendentals=0
-        ),
-        name="mixing",
-    )(q, k, v, z, bd, wc, gain, wout)
-
-
-def transcoder_kernel(
-    part_ref, res_ref, gain_ref, benc_ref, bdec_ref, wenc_hbm, wdec_hbm,
-    out_ref,
-    wenc, wdec, arrived, streams, normed, latents, decoded, returned,
-    wsem, s1, r1, s2, r2, s3, r3,
-):
-    me = lax.axis_index("lat")
-    load_enc = pltpu.make_async_copy(wenc_hbm, wenc, wsem.at[0])
-    load_dec = pltpu.make_async_copy(wdec_hbm, wdec, wsem.at[1])
-    load_enc.start()
-    load_dec.start()
-
-    barrier = pltpu.get_barrier_semaphore()
-    for d in range(1, LAT):
-        peer = lax.rem(me + d, LAT)
-        pl.semaphore_signal(barrier, inc=1, device_id={"lat": peer}, device_id_type=MESH)
-    pl.semaphore_wait(barrier, LAT - 1)
-
-    def peer_at(d):
-        return lax.rem(me + d, LAT)
-
-    def scatter(d):
-        return remote(part_ref.at[peer_at(d)], arrived.at[me], s1.at[d - 1], r1.at[me], lat=peer_at(d))
-
-    def gather(d):
-        return remote(streams.at[me], streams.at[me], s2.at[d - 1], r2.at[me], lat=peer_at(d))
-
-    def scatter_back(d):
-        return remote(decoded.at[peer_at(d)], returned.at[me], s3.at[d - 1], r3.at[me], lat=peer_at(d))
-
-    for d in range(1, LAT):
-        scatter(d).start()
-    attention = part_ref[me].astype(F32)
-    for d in range(1, LAT):
-        p = peer_at(d)
-        remote(part_ref.at[p], arrived.at[p], s1.at[0], r1.at[p], lat=p).wait_recv()
-        attention = attention + arrived[p].astype(F32)
-    streams[me] = (res_ref[...].astype(F32) + attention).astype(BF16)
-    for d in range(1, LAT):
-        gather(d).start()
-    own = streams[me].astype(F32)
-    squares = jnp.sum(own * own, axis=1, keepdims=True)
-    for d in range(1, LAT):
-        p = peer_at(d)
-        remote(streams.at[p], streams.at[p], s2.at[0], r2.at[p], lat=p).wait_recv()
-        wide = streams[p].astype(F32)
-        squares = squares + jnp.sum(wide * wide, axis=1, keepdims=True)
-    scale = lax.rsqrt(squares * (1.0 / 2048.0) + EPSILON)
-    for l in range(LAT):
-        cols = slice(l * 256, (l + 1) * 256)
-        normed[:, cols] = (streams[l].astype(F32) * scale * gain_ref[:, cols]).astype(BF16)
-    load_enc.wait()
-
-    def encode(i, _):
-        cols = pl.ds(pl.multiple_of(i * 256, 256), 256)
-        pre = jnp.dot(normed[...], wenc[:, cols], preferred_element_type=F32) + benc_ref[:, cols]
-        latents[:, cols] = jnp.maximum(pre, 0.0).astype(BF16)
-        return 0
-
-    lax.fori_loop(0, LAT, encode, 0)
-    load_dec.wait()
-
-    def decode(p):
-        rows = pl.ds(pl.multiple_of(p * 256, 256), 256)
-        return lax.dot_general(
-            latents[...], wdec[rows, :], (((1,), (1,)), ((), ())), preferred_element_type=F32
-        )
-
-    def decode_step(d, _):
-        p = peer_at(d)
-        decoded[p] = decode(p).astype(BF16)
-        scatter_back(d).start()
-        return 0
-
-    lax.fori_loop(1, LAT, decode_step, 0)
-    total = decode(me) + streams[me].astype(F32) + bdec_ref[...]
-    for d in range(1, LAT):
-        p = peer_at(d)
-        remote(decoded.at[p], returned.at[p], s3.at[0], r3.at[p], lat=p).wait_recv()
-        total = total + returned[p].astype(F32)
-    out_ref[...] = total.astype(BF16)
-    for d in range(1, LAT):
-        scatter(d).wait_send()
-        gather(d).wait_send()
-        scatter_back(d).wait_send()
-
-
-def transcoder(part, residual, gain, benc, bdec, wenc, wdec):
-    vmem = pl.BlockSpec(memory_space=pltpu.VMEM)
-    block = pltpu.VMEM((LAT, T, 256), BF16)
-    return pl.pallas_call(
-        transcoder_kernel,
-        out_shape=jax.ShapeDtypeStruct((T, 256), BF16),
-        in_specs=[vmem] * 5 + [pl.BlockSpec(memory_space=pl.ANY)] * 2,
-        out_specs=vmem,
-        scratch_shapes=[
+            pltpu.VMEM((512, 2048), BF16),
             pltpu.VMEM((2048, 2048), BF16),
             pltpu.VMEM((2048, 2048), BF16),
+            block,
             block,
             block,
             pltpu.VMEM((T, 2048), BF16),
             pltpu.VMEM((T, 2048), BF16),
             block,
             block,
-            pltpu.SemaphoreType.DMA((2,)),
+            dma((3,)),
+            dma((3,)),
+            dma((H,)),
+            dma((ROW,)),
+            dma((ROWS - 1,)),
+            dma((ROWS,)),
+            dma((ROW,)),
+            dma((H,)),
+            dma((3,)),
         ]
-        + [pltpu.SemaphoreType.DMA((LAT - 1,)), pltpu.SemaphoreType.DMA((LAT,))] * 3,
+        + [dma((LAT - 1,)), dma((LAT,))] * 3
+        + [dma((2, 16)), dma((2, 16)), dma((2, 16))]
+        + [dma((2, 2)), dma((2,)), dma((2, 4, 2)), dma((2, 4))],
         compiler_params=pltpu.CompilerParams(
-            collective_id=1, has_side_effects=True, vmem_limit_bytes=VMEM_LIMIT
+            collective_id=0, has_side_effects=True, vmem_limit_bytes=VMEM_LIMIT
         ),
-        cost_estimate=pl.CostEstimate(
-            flops=6_442_450_944, bytes_accessed=20_000_000, transcendentals=0
-        ),
-        name="transcoder",
-    )(part, residual, gain, benc, bdec, wenc, wdec)
+        name="layer",
+    )(q, k, v, z, bd, wc, gain, residual, pgain, benc, bdec, wout, wenc, wdec)
 
 
 def per_device(
@@ -498,11 +592,9 @@
     bd = jnp.concatenate([beta_raw, decay_log], axis=0)
     bd = bd.reshape(8, T // C, C).transpose(1, 0, 2)
     wc = jnp.concatenate([conv_q, conv_k, conv_v], axis=1)
-    wenc = lax.all_gather(w_enc, "seq", axis=0, tiled=True)
-    wdec = lax.all_gather(w_dec, "seq", axis=0, tiled=True)
-    part = mixing(q_raw, k_raw, v_raw, z_gate, bd, wc, norm_gain[None, :], w_out)
-    return transcoder(
-        part, residual, post_gain[None, :], b_enc[None, :], b_dec[None, :], wenc, wdec
+    return layer(
+        q_raw, k_raw, v_raw, z_gate, bd, wc, norm_gain[None, :], residual, post_gain[None, :],
+        b_enc[None, :], b_dec[None, :], w_out, w_enc, w_dec,
     )
 
 

time: 264 us -> 176 us (0.67)
  waiting for transfers between devices: 111 us -> 0 us
  Pallas kernels: 135 us -> 170 us
  between operations: 13.4 us -> 0.01 us
    all_gather x2 -> x0, waiting for transfers between devices: 109 us -> none  [the longest x1 81.9 us: per_device(): wdec = lax.all_gather(w_dec, 'seq', axis=0, tiled=True)]
    pallas_call x2 -> x1, Pallas kernels: 135 us -> 170 us  [layer(): pl.pallas_call(layer_kernel, out_shape=jax.ShapeDtypeStruct((T, 256), BF1...]
  transfers between devices with their start and end apart: 2 -> 0, of which waited for: 2 -> 0; matrix products, arithmetic and copies ran while one was open for 1% -> 0% of each run, Pallas kernels for 21% -> 0%
where the time goes in v2:
time: 176 us; the launch traced here: 175 us
  Pallas kernels  170 us (97%)
  other arithmetic  2.64 us (2%)
    pallas_call x1, Pallas kernels, layer(): pl.pallas_call(layer_kernel, out_shape=jax.ShapeDtypeStruct((T, 256), BF1...  170 us

profile of v2, /device:TPU:4, one launch (start us, length us, event | category | flops | bytes accessed | tf_op | source)
XLA Modules:
  0.0 174.6 jit_solution(10690826008688847970)
XLA Ops:
  0.0 1.3 maximum_bitcast_fusion.bd_ref
  1.3 1.3 pad_maximum_fusion.wc_ref
  2.6 170.3 %layer.1 = bf16[384,256]{1,0:T(8,128)(2,1)} custom-call(bf16[384,256]{1,0:T(8,128)(2,1)} %q_ref.1, bf16[384,256]{1,0:T(8,128)(2,1)} %k_ref.1, bf16[384,512]{1,0:T(8,128)(2,1)} %v_ref.1, bf16[384,512]{1,0:T(8,128)(2,1)} %z_ref.1, f32[3,8,128]{2,1,0:T(8,128)} %maximum_bitcast_fusion.bd_ref, f32[4,1024]{1,0:T(4,128)} %pad_maximum_fusion.wc_ref, ...), custom_call_target="tpu_custom_call" | custom-call | tf_op jit(solution)/shard_map/layer/pallas_call | solution.py:520
  172.9 1.6 copy.19

commit v3 on v2

--- a/solution.py
+++ b/solution.py
@@ -73,13 +73,14 @@
 
 
 def layer_kernel(
-    q_ref, k_ref, v_ref, z_ref, bd_ref, wc_ref, gain_ref,
+    q_ref, k_ref, v_ref, z_ref, beta_ref, decay_ref, cq_ref, ck_ref, cv_ref, gain_ref,
     res_ref, pgain_ref, benc_ref, bdec_ref, wout_hbm, wenc_hbm, wdec_hbm,
     out_ref,
-    halo, pad, qs, ks, vs, ql, ol, comp, acur, msg, slots, prefix, aprefix, tot, tslots, sout, sin,
-    wout_ref, wenc, wdec, part_ref, arrived, streams, normed, latents, decoded, returned,
+    bds, halo, pad, qs, ks, vs, ql, ol, comp, acur, msg, slots, prefix, aprefix, tot, tslots, sout, sin,
+    wout_ref, wenc, wdec, part, streams, normed, latents, decoded,
+    xarr1, zsend1, zrecv1, zarr1, xsend1, xrecv1, xarr2, zsend2, zrecv2, zarr2, xsend2, xrecv2,
     hs, hr, ms, mr, ts, tr, ss, sr,
-    wsem, s1, r1, s2, r2, s3, r3,
+    wsem, xs1, xr1, zs1, zr1, xs2, xr2, zs2, zr2, gxs, gzs, ga, gr_lat,
     gr, cr, cs, z1s, z2s, y1s, y2s,
 ):
     seq = lax.axis_index("seq")
@@ -110,62 +111,81 @@
     def shard_id(dy, dz):
         return lax.rem(y + dy, ROWS) * 4 + lax.rem(zh + dz, 4)
 
-    def shard(a, s, c):
-        return full[a].at[pl.ds(pl.multiple_of((s * 2 + c) * 64, 64), 64), :]
+    def shard(a, s, c, half=None):
+        lo, size = (0, 64) if half is None else (32 * half, 32)
+        return full[a].at[pl.ds(pl.multiple_of((s * 2 + c) * 64 + lo, 32), size), :]
 
     def seq_at(dy, dz):
         return shard_id(dy, dz) * 2 + core
 
-    def passed(a, s, sem, to):
-        return remote(shard(a, s, core), shard(a, s, core), sem, gr.at[a, s], seq=to)
+    def passed(a, s, sem, to, half=None):
+        block = shard(a, s, core, half)
+        return remote(block, block, sem, gr.at[a, half or 0, s], seq=to)
 
     def along_z(a, up):
-        to = seq_at(0, 1 if up else 3)
-        here = shard(a, shard_id(0, 0), core)
-        return remote(own_shard[a], here, z1s.at[a, int(up)], gr.at[a, shard_id(0, 0)], seq=to)
-
-    def along_z_on(a):
-        return passed(a, shard_id(0, 3 if a == 0 else 1), z2s.at[a], seq_at(0, 1 if a == 0 else 3))
+        s, sem = shard_id(0, 0), z1s.at[a, up]
+        return remote(
+            own_shard[a], shard(a, s, core), sem, gr.at[a, 0, s], seq=seq_at(0, 1 if up else 3)
+        )
+
+    def along_z_on(a, half):
+        s, to = (shard_id(0, 3), seq_at(0, 1)) if half == 0 else (shard_id(0, 1), seq_at(0, 3))
+        return passed(a, s, z2s.at[a, half], to, half)
 
     def along_y(a, dz, up):
-        s, to, sem = shard_id(0, dz), seq_at(1 if up else 3, 0), y1s.at[a, dz, int(up)]
+        s, to, sem = shard_id(0, dz), seq_at(1 if up else 3, 0), y1s.at[a, dz, up]
         if dz == 0:
-            return remote(own_shard[a], shard(a, s, core), sem, gr.at[a, s], seq=to)
+            return remote(own_shard[a], shard(a, s, core), sem, gr.at[a, 0, s], seq=to)
         return passed(a, s, sem, to)
 
-    def along_y_on(a, dz):
-        s = shard_id(3 if a == 0 else 1, dz)
-        return passed(a, s, y2s.at[a, dz], seq_at(1 if a == 0 else 3, 0))
+    def along_y_on(a, dz, half):
+        s, to = (shard_id(3, dz), seq_at(1, 0)) if half == 0 else (shard_id(1, dz), seq_at(3, 0))
+        return passed(a, s, y2s.at[a, dz, half], to, half)
 
     def across(a, dy, dz):
         s = shard_id(dy, dz)
         src = own_shard[a] if dy == 0 and dz == 0 else shard(a, s, core)
         return remote(src, shard(a, s, core), cs.at[a, s], cr.at[a, s], seq=sibling)
 
-    def landed(a, dy, dz):
+    def landed(a, dy, dz, half=None):
         s = shard_id(dy, dz)
-        remote(shard(a, s, core), shard(a, s, core), cs.at[a, s], gr.at[a, s], seq=sibling).wait_recv()
+        passed(a, s, cs.at[a, s], sibling, half).wait_recv()
 
     def landed_across(a, dy, dz):
         s = shard_id(dy, dz)
         there = shard(a, s, 1 - core)
         remote(there, there, cs.at[a, s], cr.at[a, s], seq=sibling).wait_recv()
 
-    def from_z(a, dz):
-        landed(a, 0, dz)
-        along_y(a, dz, True).start()
-        along_y(a, dz, False).start()
+    def start_z(a):
+        for up in range(2):
+            along_z(a, up).start()
+
+    def start_y(a, dz):
+        for up in range(2):
+            along_y(a, dz, up).start()
         across(a, 0, dz).start()
 
+    def from_z(a):
+        for half, dz in enumerate((3, 1)):
+            landed(a, 0, dz)
+            along_z_on(a, half).start()
+        start_y(a, 3)
+        start_y(a, 1)
+
+    def from_z_on(a):
+        for half in range(2):
+            landed(a, 0, 2, half)
+        start_y(a, 2)
+
     def from_y(a, dz):
-        for dy in (3, 1) if a == 0 else (1, 3):
+        for half, dy in enumerate((3, 1)):
             landed(a, dy, dz)
-            if dy == (3 if a == 0 else 1):
-                along_y_on(a, dz).start()
+            along_y_on(a, dz, half).start()
             across(a, dy, dz).start()
 
     def from_y_on(a, dz):
-        landed(a, 2, dz)
+        for half in range(2):
+            landed(a, 2, dz, half)
         across(a, 2, dz).start()
 
     loads = [
@@ -184,22 +204,24 @@
         )
         halos[-1].start()
         pad[pl.ds(16, T), lo : lo + width] = ref[...].astype(F32)
-    for a in range(2):
-        for up in (True, False):
-            along_z(a, up).start()
-            along_y(a, 0, up).start()
-        across(a, 0, 0).start()
+    start_z(0)
+    start_y(0, 0)
+    start_y(1, 0)
     for copy in loads:
         copy.start()
     for copy in halos:
         copy.wait()
     pad[pl.ds(0, 16), :] = jnp.where(seq == 0, 0.0, halo[...].astype(F32))
 
+    bds[0:4, :] = beta_ref[...]
+    bds[4:8, :] = decay_ref[...]
     for g in range(8):
         cols = slice(g * W, (g + 1) * W)
-        total = wc_ref[0:1, cols] * pad[13 : 13 + T, cols]
+        taps = (cq_ref, ck_ref, cv_ref)[min(g // 2, 2)]
+        lo = (g - 2 * min(g // 2, 2)) * W
+        total = taps[0:1, lo : lo + W] * pad[13 : 13 + T, cols]
         for tap in range(1, 4):
-            total = total + wc_ref[tap : tap + 1, cols] * pad[13 + tap : 13 + tap + T, cols]
+            total = total + taps[tap : tap + 1, lo : lo + W] * pad[13 + tap : 13 + tap + T, cols]
         total = silu(total)
         if g < 4:
             total = total * lax.rsqrt(jnp.sum(total * total, axis=1, keepdims=True) + EPSILON)
@@ -210,10 +232,6 @@
         else:
             vs[:, (g - 4) * W : (g - 3) * W] = total
 
-    from_z(0, 3)
-    along_z_on(0).start()
-    from_z(0, 1)
-
     row = lax.broadcasted_iota(jnp.int32, (C, C), 0)
     col = lax.broadcasted_iota(jnp.int32, (C, C), 1)
     lower = (col <= row).astype(F32)
@@ -225,7 +243,7 @@
 
     def block(c, _):
         rows = pl.ds(pl.multiple_of(c * C, C), C)
-        bd = bd_ref[c]
+        bd = bds[:, rows]
         beta_col = mm6(eye, 1.0 / (1.0 + jnp.exp(-bd)), ((1,), (1,)))
         cum_col = mm6(lower, bd, ((1,), (1,)))
         cum_row = mm6(bd, upper)
@@ -275,16 +293,13 @@
 
         @pl.when(c == 0)
         def _():
-            from_z(1, 1)
-            along_z_on(1).start()
-            from_z(1, 3)
+            from_z(0)
+            start_z(1)
+
+        @pl.when(c == 1)
+        def _():
             from_y(0, 0)
             from_y(1, 0)
-
-        @pl.when(c == 1)
-        def _():
-            from_z(0, 2)
-            from_z(1, 2)
 
         return 0
 
@@ -318,8 +333,7 @@
         def _():
             slots[j] = msg[h]
 
-    from_y(0, 1)
-    from_y(0, 3)
+    from_z_on(0)
 
     def total_to(d):
         peer = lax.rem(y + d, ROWS)
@@ -356,6 +370,7 @@
         for d in range(1, ROWS):
             total_to(d).start()
         tslots[y] = tot[...]
+        from_z(1)
         state = jnp.zeros((C, W), F32)
         for i in range(ROWS):
 
@@ -389,9 +404,14 @@
             def _():
                 sin[zh] = sout[i]
 
-    from_y(1, 1)
-    from_y(1, 3)
-
+    @pl.when(core == 1)
+    def _():
+        from_z(1)
+
+    from_y(0, 3)
+    from_y(0, 1)
+    from_y_on(0, 0)
+    from_y_on(1, 0)
     gated = []
     for h in range(H):
 
@@ -406,8 +426,252 @@
     gated = jnp.concatenate(gated, axis=1)
     for copy in loads:
         copy.wait()
-    for lane in range(LAT):
-        part_ref[lane] = mm(gated, wout_ref[:, lane * 256 : (lane + 1) * 256]).astype(BF16)
+
+    zl, x = me // 4, lax.rem(me, 4)
+    other = 1 - zl
+    HALF = T // 2
+
+    def lat_at(plane, column):
+        return plane * 4 + column
+
+    def column_at(d):
+        return lax.rem(x + d, 4)
+
+    def token_rows(block):
+        return pl.ds(block * HALF, HALF)
+
+    class ColumnsFirst:
+        def __init__(self, src, rows, bufs, sems):
+            self.src, self.rows = src, rows
+            self.xarr, self.zsend, self.zrecv = bufs
+            self.xs, self.xr, self.zs, self.zr = sems
+
+        def to_column(self, d):
+            c = column_at(d)
+            return remote(
+                self.src.at[:, c, self.rows, :], self.xarr.at[:, x],
+                self.xs.at[d - 1], self.xr.at[x], lat=lat_at(zl, c),
+            )
+
+        def to_plane(self):
+            return remote(self.zsend, self.zrecv, self.zs.at[0], self.zr.at[0], lat=lat_at(other, x))
+
+        def turn(self):
+            own = self.src[zl, x, self.rows, :].astype(F32)
+            theirs = self.src[other, x, self.rows, :].astype(F32)
+            for d in range(1, 4):
+                c = column_at(d)
+                remote(
+                    self.src.at[:, c, self.rows, :], self.xarr.at[:, c],
+                    self.xs.at[0], self.xr.at[c], lat=lat_at(zl, c),
+                ).wait_recv()
+                own = own + self.xarr[zl, c].astype(F32)
+                theirs = theirs + self.xarr[other, c].astype(F32)
+            self.zsend[...] = theirs.astype(BF16)
+            self.to_plane().start()
+            self.own = own
+
+        def finish(self):
+            self.to_plane().wait_recv()
+            return self.own + self.zrecv[...].astype(F32)
+
+        def close(self):
+            for d in range(1, 4):
+                self.to_column(d).wait_send()
+            self.to_plane().wait_send()
+
+    class PlanesFirst:
+        def __init__(self, src, rows, bufs, sems):
+            self.src, self.rows = src, rows
+            self.zarr, self.xsend, self.xrecv = bufs
+            self.xs, self.xr, self.zs, self.zr = sems
+
+        def to_plane(self):
+            return remote(
+                self.src.at[other, :, self.rows, :], self.zarr,
+                self.zs.at[0], self.zr.at[0], lat=lat_at(other, x),
+            )
+
+        def to_column(self, d):
+            c = column_at(d)
+            return remote(
+                self.xsend.at[c], self.xrecv.at[x], self.xs.at[d - 1], self.xr.at[x],
+                lat=lat_at(zl, c),
+            )
+
+        def turn(self):
+            self.to_plane().wait_recv()
+            for d in range(1, 4):
+                c = column_at(d)
+                both = self.src[zl, c, self.rows, :].astype(F32) + self.zarr[c].astype(F32)
+                self.xsend[c] = both.astype(BF16)
+                self.to_column(d).start()
+            self.own = self.src[zl, x, self.rows, :].astype(F32) + self.zarr[x].astype(F32)
+
+        def finish(self):
+            total = self.own
+            for d in range(1, 4):
+                c = column_at(d)
+                remote(
+                    self.xsend.at[c], self.xrecv.at[c], self.xs.at[0], self.xr.at[c],
+                    lat=lat_at(zl, c),
+                ).wait_recv()
+                total = total + self.xrecv[c].astype(F32)
+            return total
+
+        def close(self):
+            for d in range(1, 4):
+                self.to_column(d).wait_send()
+            self.to_plane().wait_send()
+
+    def project(block):
+        rows = gated[block * HALF : (block + 1) * HALF, :]
+        for lane in range(LAT):
+            part[lane // 4, lane % 4, token_rows(block), :] = mm(
+                rows, wout_ref[:, lane * 256 : (lane + 1) * 256]
+            ).astype(BF16)
+
+    sums1 = (
+        ColumnsFirst(part, token_rows(0), (xarr1, zsend1, zrecv1), (xs1.at[0], xr1.at[0], zs1.at[0], zr1.at[0])),
+        PlanesFirst(part, token_rows(1), (zarr1, xsend1, xrecv1), (xs1.at[1], xr1.at[1], zs1.at[1], zr1.at[1])),
+    )
+    sums2 = (
+        PlanesFirst(decoded, token_rows(0), (zarr2, xsend2, xrecv2), (xs2.at[0], xr2.at[0], zs2.at[0], zr2.at[0])),
+        ColumnsFirst(decoded, token_rows(1), (xarr2, zsend2, zrecv2), (xs2.at[1], xr2.at[1], zs2.at[1], zr2.at[1])),
+    )
+
+    def slot(block, plane, column):
+        return streams.at[plane, column, token_rows(block), :]
+
+    def give(block, plane, column, sem, **to):
+        here = slot(block, plane, column)
+        return remote(here, here, sem, gr_lat.at[block, lat_at(plane, column)], **to)
+
+    def give_own_x(block, d):
+        return give(block, zl, x, gxs.at[block, d - 1], lat=lat_at(zl, column_at(d)))
+
+    def give_own_z(block):
+        return give(block, zl, x, gzs.at[block], lat=lat_at(other, x))
+
+    def give_on(block, d):
+        if block == 0:
+            return give(0, other, x, ga.at[0, d - 1], lat=lat_at(zl, column_at(d)))
+        return give(1, zl, column_at(d), ga.at[1, d - 1], lat=lat_at(other, x))
+
+    def got(block, plane, column):
+        give(block, plane, column, gzs.at[block], lat=lat_at(other, x)).wait_recv()
+
+    def enter_stream(block):
+        rows = token_rows(block)
+        summed = sums1[block].finish()
+        streams[zl, x, rows, :] = (res_ref[rows, :].astype(F32) + summed).astype(BF16)
+        for d in range(1, 4):
+            give_own_x(block, d).start()
+        give_own_z(block).start()
+
+    def normalise(block):
+        rows = token_rows(block)
+        squares = jnp.zeros((HALF, 1), F32)
+        for plane in range(2):
+            for column in range(4):
+                wide = streams[plane, column, rows, :].astype(F32)
+                squares = squares + jnp.sum(wide * wide, axis=1, keepdims=True)
+        scale = lax.rsqrt(squares * (1.0 / 2048.0) + EPSILON)
+        for lane in range(LAT):
+            cols = slice(lane * 256, (lane + 1) * 256)
+            wide = streams[lane // 4, lane % 4, rows, :].astype(F32)
+            normed[rows, cols] = (wide * scale * pgain_ref[:, cols]).astype(BF16)
+
+    def encode(block):
+        rows = token_rows(block)
+
+        def step(i, _):
+            cols = pl.ds(pl.multiple_of(i * 256, 256), 256)
+            pre = jnp.dot(normed[rows, :], wenc[:, cols], preferred_element_type=F32)
+            latents[rows, cols] = jnp.maximum(pre + benc_ref[:, cols], 0.0).astype(BF16)
+            return 0
+
+        lax.fori_loop(0, LAT, step, 0)
+
+    def decode(block, plane, column):
+        rows = token_rows(block)
+        features = pl.ds(pl.multiple_of(lat_at(plane, column) * 256, 256), 256)
+        decoded[plane, column, rows, :] = lax.dot_general(
+            latents[rows, :], wdec[features, :], (((1,), (1,)), ((), ())),
+            preferred_element_type=F32,
+        ).astype(BF16)
+
+    def leave(block):
+        rows = token_rows(block)
+        total = sums2[block].finish() + streams[zl, x, rows, :].astype(F32) + bdec_ref[...]
+        out_ref[rows, :] = total.astype(BF16)
+
+    project(0)
+    for d in range(1, 4):
+        sums1[0].to_column(d).start()
+    project(1)
+    sums1[1].to_plane().start()
+    from_z_on(1)
+    from_y(0, 2)
+    sums1[0].turn()
+    sums1[1].turn()
+    from_y(1, 3)
+    from_y(1, 1)
+    enter_stream(0)
+    enter_stream(1)
+    for dz in range(1, 4):
+        from_y_on(0, dz)
+    got(0, other, x)
+    for d in range(1, 4):
+        give_on(0, d).start()
+    for d in range(1, 4):
+        got(1, zl, column_at(d))
+        give_on(1, d).start()
+    from_y(1, 2)
+    for d in range(1, 4):
+        got(0, zl, column_at(d))
+    for d in range(1, 4):
+        got(0, other, column_at(d))
+    normalise(0)
+    for dy in range(4):
+        for dz in range(4):
+            landed_across(0, dy, dz)
+    encode(0)
+    for dz in range(1, 4):
+        from_y_on(1, dz)
+    for dy in range(4):
+        for dz in range(4):
+            landed_across(1, dy, dz)
+
+    def other_plane(i, _):
+        decode(0, other, i)
+        return 0
+
+    def own_plane(i, _):
+        decode(0, zl, i)
+        return 0
+
+    lax.fori_loop(0, 4, other_plane, 0)
+    sums2[0].to_plane().start()
+    lax.fori_loop(0, 4, own_plane, 0)
+    for d in range(4):
+        got(1, other, column_at(d))
+    normalise(1)
+    encode(1)
+    sums2[0].turn()
+
+    def both_planes(d, _):
+        decode(1, 0, column_at(d))
+        decode(1, 1, column_at(d))
+        return 0
+
+    for d in range(1, 4):
+        both_planes(d, 0)
+        sums2[1].to_column(d).start()
+    both_planes(0, 0)
+    leave(0)
+    sums2[1].turn()
+    leave(1)
 
     for h in range(H):
 
@@ -425,104 +689,36 @@
             def _():
                 state_to(i).wait_send()
 
-    def peer_at(d):
-        return lax.rem(me + d, LAT)
-
-    def scatter(d):
-        return remote(part_ref.at[peer_at(d)], arrived.at[me], s1.at[d - 1], r1.at[me], lat=peer_at(d))
-
-    def gather(d):
-        return remote(streams.at[me], streams.at[me], s2.at[d - 1], r2.at[me], lat=peer_at(d))
-
-    def scatter_back(d):
-        return remote(decoded.at[peer_at(d)], returned.at[me], s3.at[d - 1], r3.at[me], lat=peer_at(d))
-
-    for d in range(1, LAT):
-        scatter(d).start()
-    from_y(0, 2)
-    from_y(1, 2)
-    attention = part_ref[me].astype(F32)
-    for d in range(1, LAT):
-        p = peer_at(d)
-        remote(part_ref.at[p], arrived.at[p], s1.at[0], r1.at[p], lat=p).wait_recv()
-        attention = attention + arrived[p].astype(F32)
-    streams[me] = (res_ref[...].astype(F32) + attention).astype(BF16)
-    for d in range(1, LAT):
-        gather(d).start()
-    for dz in range(4):
-        for a in range(2):
-            from_y_on(a, dz)
-    own = streams[me].astype(F32)
-    squares = jnp.sum(own * own, axis=1, keepdims=True)
-    for d in range(1, LAT):
-        p = peer_at(d)
-        remote(streams.at[p], streams.at[p], s2.at[0], r2.at[p], lat=p).wait_recv()
-        wide = streams[p].astype(F32)
-        squares = squares + jnp.sum(wide * wide, axis=1, keepdims=True)
-    scale = lax.rsqrt(squares * (1.0 / 2048.0) + EPSILON)
-    for l in range(LAT):
-        cols = slice(l * 256, (l + 1) * 256)
-        normed[:, cols] = (streams[l].astype(F32) * scale * pgain_ref[:, cols]).astype(BF16)
-    for dy in range(4):
+    for sums in sums1 + sums2:
+        sums.close()
+    for block in range(2):
+        for d in range(1, 4):
+            give_own_x(block, d).wait_send()
+            give_on(block, d).wait_send()
+        give_own_z(block).wait_send()
+    for a in range(2):
+        for side in range(2):
+            along_z(a, side).wait_send()
+            along_z_on(a, side).wait_send()
         for dz in range(4):
-            landed_across(0, dy, dz)
-
-    def encode(i, _):
-        cols = pl.ds(pl.multiple_of(i * 256, 256), 256)
-        pre = jnp.dot(normed[...], wenc[:, cols], preferred_element_type=F32) + benc_ref[:, cols]
-        latents[:, cols] = jnp.maximum(pre, 0.0).astype(BF16)
-        return 0
-
-    lax.fori_loop(0, LAT, encode, 0)
-    for dy in range(4):
-        for dz in range(4):
-            landed_across(1, dy, dz)
-
-    def decode(p):
-        rows = pl.ds(pl.multiple_of(p * 256, 256), 256)
-        return lax.dot_general(
-            latents[...], wdec[rows, :], (((1,), (1,)), ((), ())), preferred_element_type=F32
-        )
-
-    def decode_step(d, _):
-        p = peer_at(d)
-        decoded[p] = decode(p).astype(BF16)
-        scatter_back(d).start()
-        return 0
-
-    lax.fori_loop(1, LAT, decode_step, 0)
-    total = decode(me) + streams[me].astype(F32) + bdec_ref[...]
-    for d in range(1, LAT):
-        p = peer_at(d)
-        remote(decoded.at[p], returned.at[p], s3.at[0], r3.at[p], lat=p).wait_recv()
-        total = total + returned[p].astype(F32)
-    out_ref[...] = total.astype(BF16)
-    for d in range(1, LAT):
-        scatter(d).wait_send()
-        gather(d).wait_send()
-        scatter_back(d).wait_send()
-    for a in range(2):
-        for up in (True, False):
-            along_z(a, up).wait_send()
-        along_z_on(a).wait_send()
-        for dz in range(4):
-            for up in (True, False):
-                along_y(a, dz, up).wait_send()
-            along_y_on(a, dz).wait_send()
+            for side in range(2):
+                along_y(a, dz, side).wait_send()
+                along_y_on(a, dz, side).wait_send()
             for dy in range(4):
                 across(a, dy, dz).wait_send()
 
 
-def layer(q, k, v, z, bd, wc, gain, residual, pgain, benc, bdec, wout, wenc, wdec):
+def layer(*args):
     vmem = pl.BlockSpec(memory_space=pltpu.VMEM)
-    block = pltpu.VMEM((LAT, T, 256), BF16)
+    block = pltpu.VMEM((2, 4, T, 256), BF16)
     dma = pltpu.SemaphoreType.DMA
     return pl.pallas_call(
         layer_kernel,
         out_shape=jax.ShapeDtypeStruct((T, 256), BF16),
-        in_specs=[vmem] * 11 + [pl.BlockSpec(memory_space=pl.ANY)] * 3,
+        in_specs=[vmem] * 14 + [pl.BlockSpec(memory_space=pl.ANY)] * 3,
         out_specs=vmem,
         scratch_shapes=[
+            pltpu.VMEM((8, T), F32),
             pltpu.VMEM((16, 1024), BF16),
             pltpu.VMEM((T + 16, 1024), F32),
             pltpu.VMEM((T, 256), F32),
@@ -545,11 +741,20 @@
             pltpu.VMEM((2048, 2048), BF16),
             block,
             block,
-            block,
             pltpu.VMEM((T, 2048), BF16),
             pltpu.VMEM((T, 2048), BF16),
             block,
-            block,
+        ]
+        + [
+            pltpu.VMEM((2, 4, T // 2, 256), BF16),
+            pltpu.VMEM((T // 2, 256), BF16),
+            pltpu.VMEM((T // 2, 256), BF16),
+            pltpu.VMEM((4, T // 2, 256), BF16),
+            pltpu.VMEM((4, T // 2, 256), BF16),
+            pltpu.VMEM((4, T // 2, 256), BF16),
+        ]
+        * 2
+        + [
             dma((3,)),
             dma((3,)),
             dma((H,)),
@@ -560,14 +765,15 @@
             dma((H,)),
             dma((3,)),
         ]
-        + [dma((LAT - 1,)), dma((LAT,))] * 3
-        + [dma((2, 16)), dma((2, 16)), dma((2, 16))]
-        + [dma((2, 2)), dma((2,)), dma((2, 4, 2)), dma((2, 4))],
+        + [dma((2, 3)), dma((2, 4)), dma((2, 1)), dma((2, 1))] * 2
+        + [dma((2, 3)), dma((2,)), dma((2, 3)), dma((2, LAT))]
+        + [dma((2, 2, 16)), dma((2, 16)), dma((2, 16))]
+        + [dma((2, 2)), dma((2, 2)), dma((2, 4, 2)), dma((2, 4, 2))],
         compiler_params=pltpu.CompilerParams(
             collective_id=0, has_side_effects=True, vmem_limit_bytes=VMEM_LIMIT
         ),
         name="layer",
-    )(q, k, v, z, bd, wc, gain, residual, pgain, benc, bdec, wout, wenc, wdec)
+    )(*args)
 
 
 def per_device(
@@ -589,12 +795,9 @@
     w_dec,
     b_dec,
 ):
-    bd = jnp.concatenate([beta_raw, decay_log], axis=0)
-    bd = bd.reshape(8, T // C, C).transpose(1, 0, 2)
-    wc = jnp.concatenate([conv_q, conv_k, conv_v], axis=1)
     return layer(
-        q_raw, k_raw, v_raw, z_gate, bd, wc, norm_gain[None, :], residual, post_gain[None, :],
-        b_enc[None, :], b_dec[None, :], w_out, w_enc, w_dec,
+        q_raw, k_raw, v_raw, z_gate, beta_raw, decay_log, conv_q, conv_k, conv_v,
+        norm_gain[None, :], residual, post_gain[None, :], b_enc[None, :], b_dec[None, :], w_out, w_enc, w_dec,
     )
 
 

time: 176 us -> 139 us (0.79)
  Pallas kernels: 170 us -> 136 us
  other arithmetic: 2.64 us -> 0 us
    pallas_call x1, Pallas kernels: 170 us -> 136 us  [layer(): pl.pallas_call(layer_kernel, out_shape=jax.ShapeDtypeStruct((T, 256), BF1...]
where the time goes in v3:
time: 139 us; the launch traced here: 138 us
  Pallas kernels  136 us (98%)
  local copies, waits for them, and re-layouts  1.62 us (1%)
    pallas_call x1, Pallas kernels, layer(): pl.pallas_call(layer_kernel, out_shape=jax.ShapeDtypeStruct((T, 256), BF1...  136 us

profile of v3, /device:TPU:4, one launch (start us, length us, event | category | flops | bytes accessed | tf_op | source)
XLA Modules:
  0.0 137.9 jit_solution(2358783035500895919)
XLA Ops:
  0.0 136.2 %layer.1 = bf16[384,256]{1,0:T(8,128)(2,1)} custom-call(bf16[384,256]{1,0:T(8,128)(2,1)} %q_ref.1, bf16[384,256]{1,0:T(8,128)(2,1)} %k_ref.1, bf16[384,512]{1,0:T(8,128)(2,1)} %v_ref.1, bf16[384,512]{1,0:T(8,128)(2,1)} %z_ref.1, f32[4,384]{1,0:T(4,128)} %beta_ref.1, f32[4,384]{1,0:T(4,128)} %decay_ref.1, f32[4,256]{1,0:T(4,128)} %cq_ref.1, f32[4,256]{1,0:T(4,128)} %ck_ref.1, ...), custom_call_target="tpu_custom_call" | custom-call | tf_op jit(solution)/shard_map/layer/pallas_call | solution.py:715
  136.3 1.6 %copy.19 = bf16[384,256]{1,0:T(8,128)(2,1)} copy(bf16[384,256]{1,0:T(8,128)(2,1)} %layer.1) | data formatting | bytes 393216

commit v4 on v3

--- a/solution.py
+++ b/solution.py
@@ -37,7 +37,10 @@
     ah, al = a
     bh, bl = b
     dot = lambda x, y: lax.dot_general(x, y, (dims, ((), ())), preferred_element_type=F32)
-    return dot(ah, bh) + (dot(ah, bl) + dot(al, bh))
+    if dims != ((1,), (0,)):
+        return dot(ah, bh) + (dot(ah, bl) + dot(al, bh))
+    both = dot(jnp.concatenate([ah, al], axis=1), jnp.concatenate([bh, bh], axis=0))
+    return both + dot(ah, bl)
 
 
 def mm6(a, b, dims=((1,), (0,))):
@@ -55,9 +58,25 @@
     for level in range(1, 7):
         block_row, block_col = row >> level, col >> level
         mask = ((block_row & 1) == 1) & (block_col == block_row - 1)
+        size = 1 << level
+        if size < 8:
+            parts = [halves(x) for x in solved]
+            below = [mm3(halves(jnp.where(mask, a, 0.0)), x) for a, x in zip(systems, parts)]
+            solved = [x - mm3(p, halves(b)) for x, p, b in zip(solved, parts, below)]
+            continue
+        shape = (C // (2 * size), 2, size, C)
+        odd = lambda m: m.reshape(shape)[:, 1].reshape(C // 2, C)
         parts = [halves(x) for x in solved]
-        below = [mm3(halves(jnp.where(mask, a, 0.0)), x) for a, x in zip(systems, parts)]
-        solved = [x - mm3(p, halves(b)) for x, p, b in zip(solved, parts, below)]
+        below = [mm3(halves(odd(jnp.where(mask, a, 0.0))), x) for a, x in zip(systems, parts)]
+        zero = jnp.zeros((C // (2 * size), 1, size, C), F32)
+        full = [
+            jnp.concatenate([zero, b.reshape(zero.shape)], axis=1).reshape(C, C) for b in below
+        ]
+        change = [mm3(halves(odd(x)), halves(f)) for x, f in zip(solved, full)]
+        solved = [
+            x - jnp.concatenate([zero, c.reshape(zero.shape)], axis=1).reshape(C, C)
+            for x, c in zip(solved, change)
+        ]
     return solved
 
 
@@ -76,7 +95,7 @@
     q_ref, k_ref, v_ref, z_ref, beta_ref, decay_ref, cq_ref, ck_ref, cv_ref, gain_ref,
     res_ref, pgain_ref, benc_ref, bdec_ref, wout_hbm, wenc_hbm, wdec_hbm,
     out_ref,
-    bds, halo, pad, qs, ks, vs, ql, ol, comp, acur, msg, slots, prefix, aprefix, tot, tslots, sout, sin,
+    bds, halo, pad, qs, ks, vs, ql, ol, msg, slots, prefix, aprefix, tot, tslots, sout, sin,
     wout_ref, wenc, wdec, part, streams, normed, latents, decoded,
     xarr1, zsend1, zrecv1, zarr1, xsend1, xrecv1, xarr2, zsend2, zrecv2, zarr2, xsend2, xrecv2,
     hs, hr, ms, mr, ts, tr, ss, sr,
@@ -112,8 +131,12 @@
         return lax.rem(y + dy, ROWS) * 4 + lax.rem(zh + dz, 4)
 
     def shard(a, s, c, half=None):
-        lo, size = (0, 64) if half is None else (32 * half, 32)
-        return full[a].at[pl.ds(pl.multiple_of((s * 2 + c) * 64 + lo, 32), size), :]
+        if half is None:
+            return full[a].at[s, c]
+        return full[a].at[s, c, pl.ds(32 * half, 32), :]
+
+    def slab(a, dy, c):
+        return full[a].at[pl.ds(lax.rem(y + dy, ROWS) * 4, 4), c]
 
     def seq_at(dy, dz):
         return shard_id(dy, dz) * 2 + core
@@ -142,19 +165,18 @@
         s, to = (shard_id(3, dz), seq_at(1, 0)) if half == 0 else (shard_id(1, dz), seq_at(3, 0))
         return passed(a, s, y2s.at[a, dz, half], to, half)
 
-    def across(a, dy, dz):
-        s = shard_id(dy, dz)
-        src = own_shard[a] if dy == 0 and dz == 0 else shard(a, s, core)
-        return remote(src, shard(a, s, core), cs.at[a, s], cr.at[a, s], seq=sibling)
+    def across(a, dy):
+        block = slab(a, dy, core)
+        return remote(block, block, cs.at[a, dy], cr.at[a, dy], seq=sibling)
 
     def landed(a, dy, dz, half=None):
         s = shard_id(dy, dz)
-        passed(a, s, cs.at[a, s], sibling, half).wait_recv()
-
-    def landed_across(a, dy, dz):
-        s = shard_id(dy, dz)
-        there = shard(a, s, 1 - core)
-        remote(there, there, cs.at[a, s], cr.at[a, s], seq=sibling).wait_recv()
+        passed(a, s, cs.at[a, 0], sibling, half).wait_recv()
+
+    def landed_across(a):
+        for dy in range(ROWS):
+            block = slab(a, dy, 1 - core)
+            remote(block, block, cs.at[a, dy], cr.at[a, dy], seq=sibling).wait_recv()
 
     def start_z(a):
         for up in range(2):
@@ -163,7 +185,6 @@
     def start_y(a, dz):
         for up in range(2):
             along_y(a, dz, up).start()
-        across(a, 0, dz).start()
 
     def from_z(a):
         for half, dz in enumerate((3, 1)):
@@ -176,17 +197,21 @@
         for half in range(2):
             landed(a, 0, 2, half)
         start_y(a, 2)
+        loads[a].wait()
+        across(a, 0).start()
 
     def from_y(a, dz):
         for half, dy in enumerate((3, 1)):
             landed(a, dy, dz)
             along_y_on(a, dz, half).start()
-            across(a, dy, dz).start()
-
-    def from_y_on(a, dz):
-        for half in range(2):
-            landed(a, 2, dz, half)
-        across(a, 2, dz).start()
+            if dz == 2:
+                across(a, dy).start()
+
+    def from_y_on(a):
+        for dz in range(4):
+            for half in range(2):
+                landed(a, 2, dz, half)
+        across(a, 2).start()
 
     loads = [
         pltpu.make_async_copy(wenc_hbm, shard(0, shard_id(0, 0), core), wsem.at[0]),
@@ -238,17 +263,15 @@
     upper = (row <= col).astype(F32)
     eye = (row == col).astype(F32)
     ones = jnp.ones((C, C), F32)
-    comp[...] = jnp.zeros_like(comp)
-    acur[...] = jnp.ones_like(acur)
-
-    def block(c, _):
-        rows = pl.ds(pl.multiple_of(c * C, C), C)
+
+    systems, scores, keys, queries, cums = [], [], [], [], []
+    for c in range(T // C):
+        rows = slice(c * C, (c + 1) * C)
         bd = bds[:, rows]
         beta_col = mm6(eye, 1.0 / (1.0 + jnp.exp(-bd)), ((1,), (1,)))
         cum_col = mm6(lower, bd, ((1,), (1,)))
         cum_row = mm6(bd, upper)
-        tot_row = mm6(bd, ones)
-        systems, scores, keys, queries = [], [], [], []
+        cums.append((beta_col, cum_col, cum_row, mm6(bd, ones)))
         for kh in range(2):
             k = ks[rows, kh * W : (kh + 1) * W]
             q = qs[rows, kh * W : (kh + 1) * W]
@@ -263,47 +286,51 @@
                 systems.append(
                     jnp.where(col < row, beta_col[:, h : h + 1] * gram * within, 0.0)
                 )
-                scores.append(score * within)
-        solved = triangular_inverses(systems, row, col)
-        key_t = [k.T for k in keys]
-        for h in range(H):
-            kh = h // 2
-            beta = beta_col[:, h : h + 1]
-            growth = jnp.exp(cum_col[:, 4 + h : 5 + h])
-            v = vs[rows, h * W : (h + 1) * W]
-            targets = jnp.concatenate([beta * v, (beta * growth) * keys[kh]], axis=1)
-            fresh = mm(solved[h], targets).astype(BF16)
-            out = mm(scores[h], fresh)
-            q_map = growth * queries[kh] - out[:, W:]
-            total = tot_row[4 + h : 5 + h, :]
-            decay = jnp.exp(total)
-            remain = jnp.exp(total - cum_row[4 + h : 5 + h, :])
-            new = mm(key_t[kh] * remain, fresh)
-            so_far = comp[h]
-            a = acur[h, 0:1, :]
-            read = mm(q_map, so_far)
-            ql[h, rows, :] = (a * q_map - read[:, W:]).astype(BF16)
-            ol[h, rows, :] = out[:, :W] + read[:, :W]
-            turned = mm(new[:, W:], so_far)
-            decay2 = jnp.concatenate([decay, decay], axis=1)
-            comp[h] = (
-                decay2 * so_far - turned + jnp.concatenate([new[:, :W], a * new[:, W:]], axis=1)
-            )
-            acur[h] = jnp.broadcast_to(a * decay, (8, W))
-
-        @pl.when(c == 0)
-        def _():
-            from_z(0)
-            start_z(1)
-
-        @pl.when(c == 1)
-        def _():
-            from_y(0, 0)
-            from_y(1, 0)
-
-        return 0
-
-    lax.fori_loop(0, T // C, block, 0)
+                scores.append((score * within).astype(BF16))
+    solved = [x.astype(BF16) for x in triangular_inverses(systems, row, col)]
+    from_z(0)
+    start_z(1)
+
+    key_t = [k.T for k in keys]
+    every = [(c, h) for c in range(T // C) for h in range(H)]
+    fresh, out, new = [], [], []
+    for i, (c, h) in enumerate(every):
+        beta_col, cum_col, _, _ = cums[c]
+        beta = beta_col[:, h : h + 1]
+        growth = jnp.exp(cum_col[:, 4 + h : 5 + h])
+        v = vs[c * C : (c + 1) * C, h * W : (h + 1) * W]
+        k = keys[2 * c + h // 2]
+        targets = jnp.concatenate([beta * v, (beta * growth) * k], axis=1)
+        fresh.append(mm(solved[i], targets).astype(BF16))
+    for i, (c, h) in enumerate(every):
+        _, _, cum_row, tot_row = cums[c]
+        remain = jnp.exp(tot_row[4 + h : 5 + h, :] - cum_row[4 + h : 5 + h, :])
+        out.append(mm(scores[i], fresh[i]))
+        new.append(mm(key_t[2 * c + h // 2] * remain, fresh[i]))
+    from_y(0, 0)
+    from_y(1, 0)
+    comp, acur = [None] * H, [None] * H
+    for i, (c, h) in enumerate(every):
+        _, cum_col, _, tot_row = cums[c]
+        rows = slice(c * C, (c + 1) * C)
+        q_map = jnp.exp(cum_col[:, 4 + h : 5 + h]) * queries[2 * c + h // 2] - out[i][:, W:]
+        decay = jnp.exp(tot_row[4 + h : 5 + h, :])
+        if c == 0:
+            ql[h, rows, :] = q_map.astype(BF16)
+            ol[h, rows, :] = out[i][:, :W]
+            comp[h], acur[h] = new[i], decay
+            continue
+        a, so_far = acur[h], comp[h]
+        read = mm(q_map, so_far)
+        ql[h, rows, :] = (a * q_map - read[:, W:]).astype(BF16)
+        ol[h, rows, :] = out[i][:, :W] + read[:, :W]
+        turned = mm(new[i][:, W:], so_far)
+        comp[h] = (
+            jnp.concatenate([decay, decay], axis=1) * so_far
+            - turned
+            + jnp.concatenate([new[i][:, :W], a * new[i][:, W:]], axis=1)
+        )
+        acur[h] = a * decay
 
     def split_row(a):
         high = a.astype(BF16).astype(F32)
@@ -318,7 +345,7 @@
 
     for h in range(H):
         msg[h, :C, :] = comp[h].astype(BF16)
-        msg[h, C:, :] = split_row(acur[h, 0:1, :])
+        msg[h, C:, :] = split_row(acur[h])
 
     def to_handler(h):
         return remote(msg.at[h], slots.at[j], ms.at[h], mr.at[j], seq=base + 2 * h)
@@ -332,8 +359,6 @@
         @pl.when(j == 2 * h)
         def _():
             slots[j] = msg[h]
-
-    from_z_on(0)
 
     def total_to(d):
         peer = lax.rem(y + d, ROWS)
@@ -370,6 +395,7 @@
         for d in range(1, ROWS):
             total_to(d).start()
         tslots[y] = tot[...]
+        from_z_on(0)
         from_z(1)
         state = jnp.zeros((C, W), F32)
         for i in range(ROWS):
@@ -406,12 +432,11 @@
 
     @pl.when(core == 1)
     def _():
+        from_z_on(0)
         from_z(1)
 
     from_y(0, 3)
     from_y(0, 1)
-    from_y_on(0, 0)
-    from_y_on(1, 0)
     gated = []
     for h in range(H):
 
@@ -424,8 +449,7 @@
         gate = silu(z_ref[:, h * W : (h + 1) * W].astype(F32))
         gated.append((delta * lax.rsqrt(squares + EPSILON) * gain_ref[...] * gate).astype(BF16))
     gated = jnp.concatenate(gated, axis=1)
-    for copy in loads:
-        copy.wait()
+    loads[2].wait()
 
     zl, x = me // 4, lax.rem(me, 4)
     other = 1 - zl
@@ -587,18 +611,17 @@
 
         def step(i, _):
             cols = pl.ds(pl.multiple_of(i * 256, 256), 256)
-            pre = jnp.dot(normed[rows, :], wenc[:, cols], preferred_element_type=F32)
+            features = wenc[:, :, :, cols].reshape(2048, 256)
+            pre = jnp.dot(normed[rows, :], features, preferred_element_type=F32)
             latents[rows, cols] = jnp.maximum(pre + benc_ref[:, cols], 0.0).astype(BF16)
             return 0
 
         lax.fori_loop(0, LAT, step, 0)
 
-    def decode(block, plane, column):
-        rows = token_rows(block)
-        features = pl.ds(pl.multiple_of(lat_at(plane, column) * 256, 256), 256)
-        decoded[plane, column, rows, :] = lax.dot_general(
-            latents[rows, :], wdec[features, :], (((1,), (1,)), ((), ())),
-            preferred_element_type=F32,
+    def decode(plane, column):
+        rows = wdec[pl.ds(lat_at(plane, column) * 2, 2)].reshape(256, 2048)
+        decoded[plane, column] = lax.dot_general(
+            latents[...], rows, (((1,), (1,)), ((), ())), preferred_element_type=F32
         ).astype(BF16)
 
     def leave(block):
@@ -619,8 +642,7 @@
     from_y(1, 1)
     enter_stream(0)
     enter_stream(1)
-    for dz in range(1, 4):
-        from_y_on(0, dz)
+    from_y_on(0)
     got(0, other, x)
     for d in range(1, 4):
         give_on(0, d).start()
@@ -633,45 +655,29 @@
     for d in range(1, 4):
         got(0, other, column_at(d))
     normalise(0)
-    for dy in range(4):
-        for dz in range(4):
-            landed_across(0, dy, dz)
+    landed_across(0)
     encode(0)
-    for dz in range(1, 4):
-        from_y_on(1, dz)
-    for dy in range(4):
-        for dz in range(4):
-            landed_across(1, dy, dz)
-
-    def other_plane(i, _):
-        decode(0, other, i)
-        return 0
-
-    def own_plane(i, _):
-        decode(0, zl, i)
-        return 0
-
-    lax.fori_loop(0, 4, other_plane, 0)
-    sums2[0].to_plane().start()
-    lax.fori_loop(0, 4, own_plane, 0)
+    from_y_on(1)
     for d in range(4):
         got(1, other, column_at(d))
     normalise(1)
     encode(1)
-    sums2[0].turn()
-
-    def both_planes(d, _):
-        decode(1, 0, column_at(d))
-        decode(1, 1, column_at(d))
+    landed_across(1)
+
+    def other_plane(i, _):
+        decode(other, i)
         return 0
 
-    for d in range(1, 4):
-        both_planes(d, 0)
+    lax.fori_loop(0, 4, other_plane, 0)
+    sums2[0].to_plane().start()
+
+    def own_plane(d, _):
+        decode(zl, column_at(d))
         sums2[1].to_column(d).start()
-    both_planes(0, 0)
-    leave(0)
-    sums2[1].turn()
-    leave(1)
+        return 0
+
+    lax.fori_loop(1, 4, own_plane, 0)
+    decode(zl, x)
 
     for h in range(H):
 
@@ -689,7 +695,7 @@
             def _():
                 state_to(i).wait_send()
 
-    for sums in sums1 + sums2:
+    for sums in sums1:
         sums.close()
     for block in range(2):
         for d in range(1, 4):
@@ -704,8 +710,14 @@
             for side in range(2):
                 along_y(a, dz, side).wait_send()
                 along_y_on(a, dz, side).wait_send()
-            for dy in range(4):
-                across(a, dy, dz).wait_send()
+        for dy in range(ROWS):
+            across(a, dy).wait_send()
+    sums2[0].turn()
+    sums2[1].turn()
+    leave(0)
+    leave(1)
+    for sums in sums2:
+        sums.close()
 
 
 def layer(*args):
@@ -726,8 +738,6 @@
             pltpu.VMEM((T, 512), F32),
             pltpu.VMEM((H, T, W), BF16),
             pltpu.VMEM((H, T, W), F32),
-            pltpu.VMEM((H, C, 2 * W), F32),
-            pltpu.VMEM((H, 8, W), F32),
             pltpu.VMEM((H, C + 16, 2 * W), BF16),
             pltpu.VMEM((ROW, C + 16, 2 * W), BF16),
             pltpu.VMEM((ROW, C, 2 * W), F32),
@@ -737,8 +747,8 @@
             pltpu.VMEM((ROW, C, W), BF16),
             pltpu.VMEM((H, C, W), BF16),
             pltpu.VMEM((512, 2048), BF16),
-            pltpu.VMEM((2048, 2048), BF16),
-            pltpu.VMEM((2048, 2048), BF16),
+            pltpu.VMEM((16, 2, 64, 2048), BF16),
+            pltpu.VMEM((16, 2, 64, 2048), BF16),
             block,
             block,
             pltpu.VMEM((T, 2048), BF16),
@@ -767,7 +777,7 @@
         ]
         + [dma((2, 3)), dma((2, 4)), dma((2, 1)), dma((2, 1))] * 2
         + [dma((2, 3)), dma((2,)), dma((2, 3)), dma((2, LAT))]
-        + [dma((2, 2, 16)), dma((2, 16)), dma((2, 16))]
+        + [dma((2, 2, 16)), dma((2, 4)), dma((2, 4))]
         + [dma((2, 2)), dma((2, 2)), dma((2, 4, 2)), dma((2, 4, 2))],
         compiler_params=pltpu.CompilerParams(
             collective_id=0, has_side_effects=True, vmem_limit_bytes=VMEM_LIMIT

time: 139 us -> 129 us (0.928)
  Pallas kernels: 136 us -> 125 us
    pallas_call x1, Pallas kernels: 136 us -> 125 us  [layer(): pl.pallas_call(layer_kernel, out_shape=jax.ShapeDtypeStruct((T, 256), BF1...]
where the time goes in v4:
time: 129 us; the launch traced here: 127 us
  Pallas kernels  125 us (97%)
  local copies, waits for them, and re-layouts  1.62 us (1%)
    pallas_call x1, Pallas kernels, layer(): pl.pallas_call(layer_kernel, out_shape=jax.ShapeDtypeStruct((T, 256), BF1...  125 us

profile of v4, /device:TPU:4, one launch (start us, length us, event | category | flops | bytes accessed | tf_op | source)
XLA Modules:
  0.0 126.8 jit_solution(15205376874560724877)
XLA Ops:
  0.0 125.1 %layer.1 = bf16[384,256]{1,0:T(8,128)(2,1)} custom-call(bf16[384,256]{1,0:T(8,128)(2,1)} %q_ref.1, bf16[384,256]{1,0:T(8,128)(2,1)} %k_ref.1, bf16[384,512]{1,0:T(8,128)(2,1)} %v_ref.1, bf16[384,512]{1,0:T(8,128)(2,1)} %z_ref.1, f32[4,384]{1,0:T(4,128)} %beta_ref.1, f32[4,384]{1,0:T(4,128)} %decay_ref.1, f32[4,256]{1,0:T(4,128)} %cq_ref.1, f32[4,256]{1,0:T(4,128)} %ck_ref.1, ...), custom_call_target="tpu_custom_call" | custom-call | tf_op jit(solution)/shard_map/layer/pallas_call | solution.py:727
  125.1 1.6 %copy.19 = bf16[384,256]{1,0:T(8,128)(2,1)} copy(bf16[384,256]{1,0:T(8,128)(2,1)} %layer.1) | data formatting | bytes 393216

commit v5 on v4

--- a/solution.py
+++ b/solution.py
@@ -289,7 +289,6 @@
                 scores.append((score * within).astype(BF16))
     solved = [x.astype(BF16) for x in triangular_inverses(systems, row, col)]
     from_z(0)
-    start_z(1)
 
     key_t = [k.T for k in keys]
     every = [(c, h) for c in range(T // C) for h in range(H)]
@@ -396,7 +395,7 @@
             total_to(d).start()
         tslots[y] = tot[...]
         from_z_on(0)
-        from_z(1)
+        start_z(1)
         state = jnp.zeros((C, W), F32)
         for i in range(ROWS):
 
@@ -432,8 +431,8 @@
 
     @pl.when(core == 1)
     def _():
+        start_z(1)
         from_z_on(0)
-        from_z(1)
 
     from_y(0, 3)
     from_y(0, 1)
@@ -444,6 +443,8 @@
         def _():
             remote(sout.at[0], sin.at[h], ss.at[0], sr.at[h], seq=base + 2 * h).wait_recv()
 
+    from_z(1)
+    for h in range(H):
         delta = ol[h] + mm(ql[h], sin[h])
         squares = jnp.mean(delta * delta, axis=1, keepdims=True)
         gate = silu(z_ref[:, h * W : (h + 1) * W].astype(F32))

time: 129 us -> 121 us (0.938); the launches traced: 127 us -> 121 us
  Pallas kernels: 125 us -> 119 us
    pallas_call x1, Pallas kernels: 125 us -> 119 us  [layer(): pl.pallas_call(layer_kernel, out_shape=jax.ShapeDtypeStruct((T, 256), BF1...]
where the time goes in v5:
time: 121 us
  Pallas kernels  119 us (98%)
  local copies, waits for them, and re-layouts  1.62 us (1%)
    pallas_call x1, Pallas kernels, layer(): pl.pallas_call(layer_kernel, out_shape=jax.ShapeDtypeStruct((T, 256), BF1...  119 us

profile of v5, /device:TPU:4, one launch (start us, length us, event | category | flops | bytes accessed | tf_op | source)
XLA Modules:
  0.0 120.8 jit_solution(13099492419419099882)
XLA Ops:
  0.0 119.2 %layer.1 = bf16[384,256]{1,0:T(8,128)(2,1)} custom-call(bf16[384,256]{1,0:T(8,128)(2,1)} %q_ref.1, bf16[384,256]{1,0:T(8,128)(2,1)} %k_ref.1, bf16[384,512]{1,0:T(8,128)(2,1)} %v_ref.1, bf16[384,512]{1,0:T(8,128)(2,1)} %z_ref.1, f32[4,384]{1,0:T(4,128)} %beta_ref.1, f32[4,384]{1,0:T(4,128)} %decay_ref.1, f32[4,256]{1,0:T(4,128)} %cq_ref.1, f32[4,256]{1,0:T(4,128)} %ck_ref.1, ...), custom_call_target="tpu_custom_call" | custom-call | tf_op jit(solution)/shard_map/layer/pallas_call | solution.py:728
  119.2 1.6 %copy.19 = bf16[384,256]{1,0:T(8,128)(2,1)} copy(bf16[384,256]{1,0:T(8,128)(2,1)} %layer.1) | data formatting | bytes 393216

commit v6 on v5

--- a/solution.py
+++ b/solution.py
@@ -436,6 +436,7 @@
 
     from_y(0, 3)
     from_y(0, 1)
+    from_z(1)
     gated = []
     for h in range(H):
 
@@ -443,7 +444,6 @@
         def _():
             remote(sout.at[0], sin.at[h], ss.at[0], sr.at[h], seq=base + 2 * h).wait_recv()
 
-    from_z(1)
     for h in range(H):
         delta = ol[h] + mm(ql[h], sin[h])
         squares = jnp.mean(delta * delta, axis=1, keepdims=True)

time: 121 us -> 120 us (level); the launches traced: 121 us -> 117 us
  Pallas kernels: 119 us -> 116 us
    pallas_call x1, Pallas kernels: 119 us -> 116 us  [layer(): pl.pallas_call(layer_kernel, out_shape=jax.ShapeDtypeStruct((T, 256), BF1...]
where the time goes in v6:
time: 120 us; the launch traced here: 117 us
  Pallas kernels  116 us (97%)
  local copies, waits for them, and re-layouts  1.62 us (1%)
    pallas_call x1, Pallas kernels, layer(): pl.pallas_call(layer_kernel, out_shape=jax.ShapeDtypeStruct((T, 256), BF1...  116 us

profile of v6, /device:TPU:4, one launch (start us, length us, event | category | flops | bytes accessed | tf_op | source)
XLA Modules:
  0.0 117.4 jit_solution(3790656460398862237)
XLA Ops:
  0.0 115.8 %layer.1 = bf16[384,256]{1,0:T(8,128)(2,1)} custom-call(bf16[384,256]{1,0:T(8,128)(2,1)} %q_ref.1, bf16[384,256]{1,0:T(8,128)(2,1)} %k_ref.1, bf16[384,512]{1,0:T(8,128)(2,1)} %v_ref.1, bf16[384,512]{1,0:T(8,128)(2,1)} %z_ref.1, f32[4,384]{1,0:T(4,128)} %beta_ref.1, f32[4,384]{1,0:T(4,128)} %decay_ref.1, f32[4,256]{1,0:T(4,128)} %cq_ref.1, f32[4,256]{1,0:T(4,128)} %ck_ref.1, ...), custom_call_target="tpu_custom_call" | custom-call | tf_op jit(solution)/shard_map/layer/pallas_call | solution.py:728
  115.8 1.6 %copy.19 = bf16[384,256]{1,0:T(8,128)(2,1)} copy(bf16[384,256]{1,0:T(8,128)(2,1)} %layer.1) | data formatting | bytes 393216
